TPU v7x, 128 devices: a whole 4x4x4 slice. The times are simulated.
128 devices in a mesh: wide: 16 (over y, x), narrow: 8 (over z, core).
Axes of the slice: x: 4, y: 4, z: 4, core: 2. Of those that a mesh axis runs over, the one named last changes fastest.
Arguments:
- tokens: int32 [4, 384], replicated, may hold values from 0 to 32
- segments: int32 [4, 384], replicated, may hold values from 0 to 5
- targets: int32 [4, 384, 384], P(None, 'wide', 'narrow'), may hold values from 0 to 63
- embed: float32 [33, 1024], P(None, ('wide', 'narrow')), may hold values from -6 to 6
- w_ab: float32 [1024, 64], P(('wide', 'narrow')), may hold values from -0.1875 to 0.1875
- w_outer: float32 [1024, 128], P(('wide', 'narrow')), may hold values from -0.1875 to 0.1875
- w_tri: float32 [128, 640], P(('wide', 'narrow')), may hold values from -0.5 to 0.5
- w_mix: float32 [128, 128], P(('wide', 'narrow')), may hold values from -0.5 to 0.5
- w_dist: float32 [128, 64], P(('wide', 'narrow')), may hold values from -0.5 to 0.5
- gains: float32 [2, 128], P(None, ('wide', 'narrow')), may hold values from 0.5 to 1.5
- m_embed: float32 [33, 1024], P(None, ('wide', 'narrow')), may hold values from -2.861023e-06 to 2.861023e-06
- m_ab: float32 [1024, 64], P(('wide', 'narrow')), may hold values from -2.861023e-06 to 2.861023e-06
- m_outer: float32 [1024, 128], P(('wide', 'narrow')), may hold values from -2.861023e-06 to 2.861023e-06
- m_tri: float32 [128, 640], P(('wide', 'narrow')), may hold values from -2.861023e-06 to 2.861023e-06
- m_mix: float32 [128, 128], P(('wide', 'narrow')), may hold values from -2.861023e-06 to 2.861023e-06
- m_dist: float32 [128, 64], P(('wide', 'narrow')), may hold values from -2.861023e-06 to 2.861023e-06
- m_gains: float32 [2, 128], P(None, ('wide', 'narrow')), may hold values from -1.5258789e-05 to 1.5258789e-05
- v_embed: float32 [33, 1024], P(None, ('wide', 'narrow')), may hold values from 4e-17 to 3.2e-16
- v_ab: float32 [1024, 64], P(('wide', 'narrow')), may hold values from 1.5e-15 to 1.2e-14
- v_outer: float32 [1024, 128], P(('wide', 'narrow')), may hold values from 1.5e-15 to 1.2e-14
- v_tri: float32 [128, 640], P(('wide', 'narrow')), may hold values from 1.5e-15 to 1.2e-14
- v_mix: float32 [128, 128], P(('wide', 'narrow')), may hold values from 1.5e-15 to 1.2e-14
- v_dist: float32 [128, 64], P(('wide', 'narrow')), may hold values from 1.5e-15 to 1.2e-14
- v_gains: float32 [2, 128], P(None, ('wide', 'narrow')), may hold values from 3e-14 to 2.4e-13
Outputs:
- loss_sum: float32 [], replicated
- pair_count: float32 [], replicated
- grad_norm: float32 [], replicated
- new_embed: float32 [33, 1024], P(None, ('wide', 'narrow'))
- new_ab: float32 [1024, 64], P(('wide', 'narrow'))
- new_outer: float32 [1024, 128], P(('wide', 'narrow'))
- new_tri: float32 [128, 640], P(('wide', 'narrow'))
- new_mix: float32 [128, 128], P(('wide', 'narrow'))
- new_dist: float32 [128, 64], P(('wide', 'narrow'))
- new_gains: float32 [2, 128], P(None, ('wide', 'narrow'))
- out_m_embed: float32 [33, 1024], P(None, ('wide', 'narrow'))
- out_m_ab: float32 [1024, 64], P(('wide', 'narrow'))
- out_m_outer: float32 [1024, 128], P(('wide', 'narrow'))
- out_m_tri: float32 [128, 640], P(('wide', 'narrow'))
- out_m_mix: float32 [128, 128], P(('wide', 'narrow'))
- out_m_dist: float32 [128, 64], P(('wide', 'narrow'))
- out_m_gains: float32 [2, 128], P(None, ('wide', 'narrow'))
- out_v_embed: float32 [33, 1024], P(None, ('wide', 'narrow'))
- out_v_ab: float32 [1024, 64], P(('wide', 'narrow'))
- out_v_outer: float32 [1024, 128], P(('wide', 'narrow'))
- out_v_tri: float32 [128, 640], P(('wide', 'narrow'))
- out_v_mix: float32 [128, 128], P(('wide', 'narrow'))
- out_v_dist: float32 [128, 64], P(('wide', 'narrow'))
- out_v_gains: float32 [2, 128], P(None, ('wide', 'narrow'))
Inputs may be any that keep to these rules, and one draw needn't show every extreme that they name: `segments`: residues of one protein may stand anywhere in the crop.
All inputs are finite; a program needn't handle non-finite values.
Results may differ from a plain program's by a relative error of at most 0.0059.
Values may be sent and summed in bfloat16 or wider, within the bound.
A program may use at most 128 MiB of HBM per device.

v0:
```python
import jax
import jax.numpy as jnp
from jax import lax
from jax.sharding import PartitionSpec as P

norm_eps = 1e-05
clip_level = 0.001
beta_one = 0.9
beta_two = 0.999
adam_eps = 1e-10
decay_rate = 0.01
step_count = 10.0
rates = (0.5, 0.016, 0.016, 0.044, 0.044, 0.044, 0.5)


def norm_forward(values, gain):
    center = values - jnp.mean(values, -1, keepdims=True)
    inverse = lax.rsqrt(jnp.mean(center * center, -1, keepdims=True) + norm_eps)
    scaled = center * inverse
    return (scaled * gain, scaled, inverse)


def norm_backward(grad_out, gain, scaled, inverse):
    grad_hat = grad_out * gain
    grad_gain = jnp.sum(grad_out * scaled, axis=(0, 1))
    first_mean = jnp.mean(grad_hat, -1, keepdims=True)
    second_mean = jnp.mean(grad_hat * scaled, -1, keepdims=True)
    return (inverse * (grad_hat - first_mean - scaled * second_mean), grad_gain)


def local(
    tokens,
    segments,
    targets,
    embed,
    w_ab,
    w_outer,
    w_tri,
    w_mix,
    w_dist,
    gains,
    m_embed,
    m_ab,
    m_outer,
    m_tri,
    m_mix,
    m_dist,
    m_gains,
    v_embed,
    v_ab,
    v_outer,
    v_tri,
    v_mix,
    v_dist,
    v_gains,
):
    masters = (embed, w_ab, w_outer, w_tri, w_mix, w_dist, gains)
    firsts = (m_embed, m_ab, m_outer, m_tri, m_mix, m_dist, m_gains)
    seconds = (v_embed, v_ab, v_outer, v_tri, v_mix, v_dist, v_gains)
    low_w = tuple((w.astype(jnp.bfloat16) for w in masters))
    full = (
        lax.all_gather(low_w[0], ("wide", "narrow"), axis=1, tiled=True),
        lax.all_gather(low_w[1], ("wide", "narrow"), axis=0, tiled=True),
        lax.all_gather(low_w[2], ("wide", "narrow"), axis=0, tiled=True),
        lax.all_gather(low_w[3], ("wide", "narrow"), axis=0, tiled=True),
        lax.all_gather(low_w[4], ("wide", "narrow"), axis=0, tiled=True),
        lax.all_gather(low_w[5], ("wide", "narrow"), axis=0, tiled=True),
        lax.all_gather(low_w[6], ("wide", "narrow"), axis=1, tiled=True),
    )
    embed_full = full[0].astype(jnp.float32)
    ab_weight = full[1]
    ab_float = ab_weight.astype(jnp.float32)
    tri_weight = full[3]
    mix_weight = full[4]
    dist_weight = full[5]
    gain_full = full[6].astype(jnp.float32)
    vocab = embed_full.shape[0]
    outer_width = ab_weight.shape[1] // 2
    pair_width = dist_weight.shape[0]
    bins = dist_weight.shape[1]
    tri_width = (tri_weight.shape[1] - pair_width) // 4
    outer_weight = full[2].reshape(outer_width, outer_width * pair_width)
    outer_float = outer_weight.astype(jnp.float32)
    length = tokens.shape[1]
    rows = targets.shape[1]
    columns = targets.shape[2]
    row_start = lax.axis_index("wide") * rows
    col_start = lax.axis_index("narrow") * columns
    highest = lax.Precision.HIGHEST
    f32 = jnp.float32
    bf16 = jnp.bfloat16
    same = (segments[:, :, None] == segments[:, None, :]).astype(f32)
    count = jnp.sum(same)

    def embed_part(tok_part):
        one_hot = (tok_part[:, None] == jnp.arange(vocab)[None, :]).astype(f32)
        return (one_hot, jnp.dot(one_hot, embed_full, precision=highest))

    def crop_step(carry, inputs):
        sums, loss_sum = carry
        tok, seg, tgt = inputs
        hot_rows, seq_rows = embed_part(lax.dynamic_slice_in_dim(tok, row_start, rows))
        ab_rows = jnp.dot(seq_rows.astype(bf16), ab_weight, preferred_element_type=f32).astype(bf16)
        left = ab_rows[:, :outer_width]
        right_all = lax.all_gather(ab_rows[:, outer_width:], "wide", axis=0, tiled=True)
        right = lax.dynamic_slice_in_dim(right_all, col_start, columns)
        inner = (
            jnp.dot(left, outer_weight, preferred_element_type=f32)
            .astype(bf16)
            .reshape(rows, outer_width, pair_width)
        )
        seg_rows = lax.dynamic_slice_in_dim(seg, row_start, rows)
        seg_cols = lax.dynamic_slice_in_dim(seg, col_start, columns)
        mask = (seg_rows[:, None] == seg_cols[None, :]).astype(f32)
        mask3 = mask[..., None]
        pair = jnp.einsum("jq,iqc->ijc", right, inner, preferred_element_type=f32) * mask3
        normed, scaled_in, inverse_in = norm_forward(pair, gain_full[0])
        normed_b = normed.astype(bf16)
        projected = jnp.einsum("ijc,cd->ijd", normed_b, tri_weight, preferred_element_type=f32)
        gate_left = jax.nn.sigmoid(projected[..., :tri_width])
        value_left = projected[..., tri_width : 2 * tri_width]
        gate_right = jax.nn.sigmoid(projected[..., 2 * tri_width : 3 * tri_width])
        value_right = projected[..., 3 * tri_width : 4 * tri_width]
        gate_out = jax.nn.sigmoid(projected[..., 4 * tri_width :])
        left_edge = (mask3 * gate_left * value_left).astype(bf16)
        right_edge = (mask3 * gate_right * value_right).astype(bf16)
        panel = lax.all_gather(right_edge, "wide", axis=0, tiled=True)
        piece = panel
        summed = lax.psum_scatter(
            jnp.einsum("jkc,ikc->jic", piece, left_edge, preferred_element_type=f32).astype(
                jnp.bfloat16
            ),
            "narrow",
            scatter_dimension=0,
            tiled=True,
        ).astype(jnp.float32)
        product = jnp.transpose(summed, (1, 0, 2))
        mixed, scaled_mid, inverse_mid = norm_forward(product, gain_full[1])
        mixed_b = mixed.astype(bf16)
        branch = jnp.einsum("ijc,cd->ijd", mixed_b, mix_weight, preferred_element_type=f32)
        update_b = (pair + gate_out * branch).astype(bf16)
        logits = jnp.einsum("ijc,ck->ijk", update_b, dist_weight, preferred_element_type=f32)
        log_prob = jax.nn.log_softmax(logits, -1)
        target_hot = (tgt[..., None] == jnp.arange(bins)).astype(f32)
        loss_sum = loss_sum - jnp.sum(mask * jnp.sum(log_prob * target_hot, -1))
        grad_logits = (mask3 * (jnp.exp(log_prob) - target_hot) / count).astype(bf16)
        grad_dist = jnp.einsum("ijc,ijk->ck", update_b, grad_logits, preferred_element_type=f32)
        grad_update = jnp.einsum(
            "ijk,ck->ijc", grad_logits, dist_weight, preferred_element_type=f32
        )
        grad_branch = (grad_update * gate_out).astype(bf16)
        grad_gate_out = grad_update * branch * gate_out * (1.0 - gate_out)
        grad_mix = jnp.einsum("ijc,ijd->cd", mixed_b, grad_branch, preferred_element_type=f32)
        grad_mixed = jnp.einsum("ijd,cd->ijc", grad_branch, mix_weight, preferred_element_type=f32)
        grad_product, grad_gain_mid = norm_backward(
            grad_mixed, gain_full[1], scaled_mid, inverse_mid
        )

        def edge_back(piece):
            grad_left = jnp.einsum("ijc,jkc->ikc", piece, panel, preferred_element_type=f32)
            term = jnp.einsum("ijc,ikc->jkc", piece, left_edge, preferred_element_type=f32)
            return (grad_left, term)

        grad_left_edge, grad_panel = edge_back(
            lax.all_gather(grad_product.astype(bf16), "narrow", axis=1, tiled=True)
        )
        grad_right_edge = lax.psum_scatter(
            grad_panel.astype(jnp.bfloat16), "wide", scatter_dimension=0, tiled=True
        ).astype(jnp.float32)
        grad_projected = jnp.concatenate(
            [
                grad_left_edge * mask3 * value_left * gate_left * (1.0 - gate_left),
                grad_left_edge * mask3 * gate_left,
                grad_right_edge * mask3 * value_right * gate_right * (1.0 - gate_right),
                grad_right_edge * mask3 * gate_right,
                grad_gate_out,
            ],
            -1,
        ).astype(bf16)
        grad_tri = jnp.einsum("ijc,ijd->cd", normed_b, grad_projected, preferred_element_type=f32)
        grad_normed = jnp.einsum(
            "ijd,cd->ijc", grad_projected, tri_weight, preferred_element_type=f32
        )
        grad_pair_in, grad_gain_in = norm_backward(grad_normed, gain_full[0], scaled_in, inverse_in)
        grad_pair = (grad_update + grad_pair_in) * mask3
        grad_inner = jnp.einsum(
            "ijc,jq->iqc", grad_pair, right.astype(f32), precision=highest
        ).reshape(rows, outer_width * pair_width)
        grad_right = jnp.einsum("ijc,iqc->jq", grad_pair, inner.astype(f32), precision=highest)
        grad_outer = jnp.dot(left.astype(f32).T, grad_inner, precision=highest).reshape(
            outer_width * outer_width, pair_width
        )
        grad_left = jnp.dot(grad_inner, outer_float.T, precision=highest)
        placed = lax.dynamic_update_slice_in_dim(
            jnp.zeros((length, outer_width), f32), grad_right, col_start, 0
        )
        grad_right_rows = lax.psum_scatter(
            placed.astype(jnp.bfloat16), "wide", scatter_dimension=0, tiled=True
        ).astype(jnp.float32)
        grad_factors = jnp.concatenate([grad_left, grad_right_rows], 1)
        grad_ab = jnp.dot(seq_rows.T, grad_factors, precision=highest)
        grad_seq = jnp.dot(grad_factors, ab_float.T, precision=highest)
        grad_embed = jnp.dot(hot_rows.T, grad_seq, precision=highest)
        grad_gains = jnp.stack([grad_gain_in, grad_gain_mid])
        terms = (grad_embed, grad_ab, grad_outer, grad_tri, grad_mix, grad_dist, grad_gains)
        sums = tuple((total + term for total, term in zip(sums, terms)))
        return ((sums, loss_sum), None)

    start_sums = tuple((jnp.zeros(w.shape, f32) for w in full))
    start_sums = (
        start_sums[0],
        start_sums[1],
        jnp.zeros((outer_width * outer_width, pair_width), f32),
        start_sums[3],
        start_sums[4],
        start_sums[5],
        start_sums[6],
    )
    (sums, loss_sum), unused = lax.scan(
        crop_step, (start_sums, jnp.zeros((), f32)), (tokens, segments, targets)
    )
    shards = (
        lax.psum_scatter(sums[0], ("wide", "narrow"), scatter_dimension=1, tiled=True),
        lax.psum_scatter(sums[1], ("wide", "narrow"), scatter_dimension=0, tiled=True),
        lax.psum_scatter(sums[2], ("wide", "narrow"), scatter_dimension=0, tiled=True),
        lax.psum_scatter(sums[3], ("wide", "narrow"), scatter_dimension=0, tiled=True),
        lax.psum_scatter(sums[4], ("wide", "narrow"), scatter_dimension=0, tiled=True),
        lax.psum_scatter(sums[5], ("wide", "narrow"), scatter_dimension=0, tiled=True),
        lax.psum_scatter(sums[6], ("wide", "narrow"), scatter_dimension=1, tiled=True),
    )
    square_sum = sum((jnp.sum(g * g) for g in shards))
    totals = lax.psum((square_sum, loss_sum), ("wide", "narrow"))
    grad_norm = jnp.sqrt(totals[0])
    loss_total = totals[1]
    scale = jnp.minimum(1.0, clip_level / grad_norm)
    news, moms, vels = ([], [], [])
    for weight, first, second, grad, rate in zip(masters, firsts, seconds, shards, rates):
        clipped = grad * scale
        first_new = beta_one * first + (1.0 - beta_one) * clipped
        second_new = beta_two * second + (1.0 - beta_two) * clipped * clipped
        ratio = (
            first_new
            / (1.0 - beta_one**step_count)
            / (jnp.sqrt(second_new / (1.0 - beta_two**step_count)) + adam_eps)
        )
        news.append(weight - rate * (ratio + decay_rate * weight))
        moms.append(first_new)
        vels.append(second_new)
    return (
        loss_total,
        count,
        grad_norm,
        news[0],
        news[1],
        news[2],
        news[3],
        news[4],
        news[5],
        news[6],
        moms[0],
        moms[1],
        moms[2],
        moms[3],
        moms[4],
        moms[5],
        moms[6],
        vels[0],
        vels[1],
        vels[2],
        vels[3],
        vels[4],
        vels[5],
        vels[6],
    )


def solution(mesh):
    return jax.shard_map(
        local,
        mesh=mesh,
        in_specs=(
            P(),
            P(),
            P(None, "wide", "narrow"),
            P(None, ("wide", "narrow")),
            P(("wide", "narrow"), None),
            P(("wide", "narrow"), None),
            P(("wide", "narrow"), None),
            P(("wide", "narrow"), None),
            P(("wide", "narrow"), None),
            P(None, ("wide", "narrow")),
            P(None, ("wide", "narrow")),
            P(("wide", "narrow"), None),
            P(("wide", "narrow"), None),
            P(("wide", "narrow"), None),
            P(("wide", "narrow"), None),
            P(("wide", "narrow"), None),
            P(None, ("wide", "narrow")),
            P(None, ("wide", "narrow")),
            P(("wide", "narrow"), None),
            P(("wide", "narrow"), None),
            P(("wide", "narrow"), None),
            P(("wide", "narrow"), None),
            P(("wide", "narrow"), None),
            P(None, ("wide", "narrow")),
        ),
        out_specs=(
            P(),
            P(),
            P(),
            P(None, ("wide", "narrow")),
            P(("wide", "narrow"), None),
            P(("wide", "narrow"), None),
            P(("wide", "narrow"), None),
            P(("wide", "narrow"), None),
            P(("wide", "narrow"), None),
            P(None, ("wide", "narrow")),
            P(None, ("wide", "narrow")),
            P(("wide", "narrow"), None),
            P(("wide", "narrow"), None),
            P(("wide", "narrow"), None),
            P(("wide", "narrow"), None),
            P(("wide", "narrow"), None),
            P(None, ("wide", "narrow")),
            P(None, ("wide", "narrow")),
            P(("wide", "narrow"), None),
            P(("wide", "narrow"), None),
            P(("wide", "narrow"), None),
            P(("wide", "narrow"), None),
            P(("wide", "narrow"), None),
            P(None, ("wide", "narrow")),
        ),
        check_vma=False,
    )
```

profile of v0, /device:TPU:1, one launch (start us, length us, event | category | flops | bytes accessed | tf_op | source)
XLA Modules:
  0.0 1993.4 jit_solution(10575134182492080402)
XLA Ops:
  14.9 34.3 %all-gather = bf16[128,1,2]{2,1,0:T(2,128)(2,1)S(1)} all-gather(bf16[1,1,2]{2,1,0:T(2,128)(2,1)S(1)} %convert_bitcast_fusion.5), channel_id=1, replica_groups=mesh['wide'=16,'narrow'=8] {'wide','narrow'}, dimensions={0}, use_global_device_ids=true | all-gather | bytes 516 | tf_op jit(solution)/shard_map/all_gather | solution.py:68
  49.9 29.6 %all-gather.3 = bf16[128,1,64]{2,1,0:T(2,128)(2,1)S(1)} all-gather(bf16[1,1,64]{2,1,0:T(2,128)(2,1)S(1)} %convert_bitcast_fusion.3), channel_id=1, replica_groups=mesh['wide'=16,'narrow'=8] {'wide','narrow'}, dimensions={0}, use_global_device_ids=true | all-gather | bytes 16512 | tf_op jit(solution)/shard_map/all_gather | solution.py:67
  80.2 29.4 %all-gather.2 = bf16[128,1,128]{2,1,0:T(2,128)(2,1)S(1)} all-gather(bf16[1,1,128]{2,1,0:T(2,128)(2,1)S(1)} %convert_bitcast_fusion.4), channel_id=1, replica_groups=mesh['wide'=16,'narrow'=8] {'wide','narrow'}, dimensions={0}, use_global_device_ids=true | all-gather | bytes 33024 | tf_op jit(solution)/shard_map/all_gather | solution.py:66
  110.2 33.2 %all_gather.43 = bf16[1024,64]{1,0:T(8,128)(2,1)S(1)} all-gather(bf16[8,64]{1,0:T(8,128)(2,1)S(1)} %convert_element_type.188), channel_id=1, replica_groups=mesh['wide'=16,'narrow'=8] {'wide','narrow'}, dimensions={0}, use_global_device_ids=true | all-gather | bytes 132096 | tf_op jit(solution)/shard_map/all_gather | solution.py:63
  143.4 33.2 %all_gather.44 = bf16[1024,128]{1,0:T(8,128)(2,1)S(1)} all-gather(bf16[8,128]{1,0:T(8,128)(2,1)S(1)} %convert_element_type.189), channel_id=1, replica_groups=mesh['wide'=16,'narrow'=8] {'wide','narrow'}, dimensions={0}, use_global_device_ids=true | all-gather | bytes 264192 | tf_op jit(solution)/shard_map/all_gather | solution.py:64
  176.7 33.3 %all_gather.42 = bf16[33,1024]{0,1:T(8,128)(2,1)S(1)} all-gather(bf16[33,8]{0,1:T(8,128)(2,1)S(1)} %convert_element_type.186), channel_id=1, replica_groups=mesh['wide'=16,'narrow'=8] {'wide','narrow'}, dimensions={1}, use_global_device_ids=true | all-gather | bytes 68112 | tf_op jit(solution)/shard_map/all_gather | solution.py:62
  210.2 33.3 %all-gather.1 = bf16[128,1,640]{2,1,0:T(2,128)(2,1)S(1)} all-gather(bf16[1,1,640]{2,1,0:T(2,128)(2,1)S(1)} %convert_bitcast_fusion.2), channel_id=1, replica_groups=mesh['wide'=16,'narrow'=8] {'wide','narrow'}, dimensions={0}, use_global_device_ids=true | all-gather | bytes 165120 | tf_op jit(solution)/shard_map/all_gather | solution.py:65
  245.8 1496.0 %while.28 = (s32[]{:T(128)}, f32[33,1024]{1,0:T(8,128)}, f32[1024,64]{0,1:T(8,128)}, f32[1024,128]{1,0:T(8,128)}, f32[128,640]{1,0:T(8,128)}, /*index=5*/f32[128...) while((s32[]{:T(128)}, f32[33,1024]{1,0:T(8,128)}, ...), condition=%wide.region_19.20_spmd.clone, body=%wide.region_1.19_spmd.clone.sunk | while | flops 1362127232 | bytes 173970704 | solution.py:219
  250.2 16.5 all_gather.55
  272.7 54.2 %all-gather.7.cloned.1.call-done = bf16[384,48,128]{2,1,0:T(8,128)(2,1)} async-done(((bf16[24,48,128]{2,1,0:T(8,128)(2,1)}), bf16[384,48,128]{2,1,0:T(8,128)(2,1)}) %all-gather.7.cloned.1.call-update) | async-done | bytes 4718608 | tf_op jit(solution)/shard_map/while/body/eval_jaxpr/all_gather | solution.py:127
  326.9 17.9 copy.214
  344.8 10.8 convert_bitcast_fusion.7
  361.5 29.7 %reduce-scatter.8.cloned.1.call-done = bf16[48,24,128]{2,1,0:T(8,128)(2,1)} async-done(((bf16[384,24,128]{2,1,0:T(8,128)(2,1)}), bf16[48,24,128]{2,1,0:T(8,128)(2,1)}) %reduce-scatter.8.cloned.1.call-update) | async-done | bytes 294928 | tf_op jit(solution)/shard_map/while/body/eval_jaxpr/reduce_scatter | solution.py:129
  407.1 28.2 %all-gather.9.cloned.1.call-done = bf16[24,384,128]{2,0,1:T(8,128)(2,1)} async-done(((bf16[24,48,128]{2,0,1:T(8,128)(2,1)}), bf16[24,384,128]{2,0,1:T(8,128)(2,1)}) %all-gather.9.cloned.1.call-update) | async-done | bytes 2359312 | tf_op jit(solution)/shard_map/while/body/eval_jaxpr/all_gather | solution.py:165
  459.7 8.9 fusion.229
  474.4 55.6 %reduce-scatter.10.cloned.1.call-done = bf16[24,48,128]{2,1,0:T(8,128)(2,1)} async-done(((bf16[384,48,128]{2,1,0:T(8,128)(2,1)}), bf16[24,48,128]{2,1,0:T(8,128)(2,1)}) %reduce-scatter.10.cloned.1.call-update) | async-done | bytes 294928 | tf_op jit(solution)/shard_map/while/body/eval_jaxpr/reduce_scatter | solution.py:167
  546.4 67.2 %reduce-scatter.12.cloned.1.call-done = bf16[24,32]{1,0:T(8,128)(2,1)} async-done(((bf16[384,32]{1,0:T(8,128)(2,1)}), bf16[24,32]{1,0:T(8,128)(2,1)}) %reduce-scatter.12.cloned.1.call-update) | async-done | bytes 1552 | tf_op jit(solution)/shard_map/while
  620.9 17.2 all_gather.55
  644.0 58.0 %all-gather.7.cloned.1.call-done = bf16[384,48,128]{2,1,0:T(8,128)(2,1)} async-done(((bf16[24,48,128]{2,1,0:T(8,128)(2,1)}), bf16[384,48,128]{2,1,0:T(8,128)(2,1)}) %all-gather.7.cloned.1.call-update) | async-done | bytes 4718608 | tf_op jit(solution)/shard_map/while/body/eval_jaxpr/all_gather | solution.py:127
  702.0 17.9 copy.214
  719.8 10.8 convert_bitcast_fusion.7
  736.6 29.7 %reduce-scatter.8.cloned.1.call-done = bf16[48,24,128]{2,1,0:T(8,128)(2,1)} async-done(((bf16[384,24,128]{2,1,0:T(8,128)(2,1)}), bf16[48,24,128]{2,1,0:T(8,128)(2,1)}) %reduce-scatter.8.cloned.1.call-update) | async-done | bytes 294928 | tf_op jit(solution)/shard_map/while/body/eval_jaxpr/reduce_scatter | solution.py:129
  782.2 28.2 %all-gather.9.cloned.1.call-done = bf16[24,384,128]{2,0,1:T(8,128)(2,1)} async-done(((bf16[24,48,128]{2,0,1:T(8,128)(2,1)}), bf16[24,384,128]{2,0,1:T(8,128)(2,1)}) %all-gather.9.cloned.1.call-update) | async-done | bytes 2359312 | tf_op jit(solution)/shard_map/while/body/eval_jaxpr/all_gather | solution.py:165
  834.8 8.9 fusion.229
  849.5 55.6 %reduce-scatter.10.cloned.1.call-done = bf16[24,48,128]{2,1,0:T(8,128)(2,1)} async-done(((bf16[384,48,128]{2,1,0:T(8,128)(2,1)}), bf16[24,48,128]{2,1,0:T(8,128)(2,1)}) %reduce-scatter.10.cloned.1.call-update) | async-done | bytes 294928 | tf_op jit(solution)/shard_map/while/body/eval_jaxpr/reduce_scatter | solution.py:167
  921.6 67.2 %reduce-scatter.12.cloned.1.call-done = bf16[24,32]{1,0:T(8,128)(2,1)} async-done(((bf16[384,32]{1,0:T(8,128)(2,1)}), bf16[24,32]{1,0:T(8,128)(2,1)}) %reduce-scatter.12.cloned.1.call-update) | async-done | bytes 1552 | tf_op jit(solution)/shard_map/while
  995.9 17.2 all_gather.55
  1019.1 58.0 %all-gather.7.cloned.1.call-done = bf16[384,48,128]{2,1,0:T(8,128)(2,1)} async-done(((bf16[24,48,128]{2,1,0:T(8,128)(2,1)}), bf16[384,48,128]{2,1,0:T(8,128)(2,1)}) %all-gather.7.cloned.1.call-update) | async-done | bytes 4718608 | tf_op jit(solution)/shard_map/while/body/eval_jaxpr/all_gather | solution.py:127
  1077.1 17.9 copy.214
  1094.9 10.8 convert_bitcast_fusion.7
  1111.7 29.7 %reduce-scatter.8.cloned.1.call-done = bf16[48,24,128]{2,1,0:T(8,128)(2,1)} async-done(((bf16[384,24,128]{2,1,0:T(8,128)(2,1)}), bf16[48,24,128]{2,1,0:T(8,128)(2,1)}) %reduce-scatter.8.cloned.1.call-update) | async-done | bytes 294928 | tf_op jit(solution)/shard_map/while/body/eval_jaxpr/reduce_scatter | solution.py:129
  1157.3 28.2 %all-gather.9.cloned.1.call-done = bf16[24,384,128]{2,0,1:T(8,128)(2,1)} async-done(((bf16[24,48,128]{2,0,1:T(8,128)(2,1)}), bf16[24,384,128]{2,0,1:T(8,128)(2,1)}) %all-gather.9.cloned.1.call-update) | async-done | bytes 2359312 | tf_op jit(solution)/shard_map/while/body/eval_jaxpr/all_gather | solution.py:165
  1195.9 7.6 copy.219
  1209.9 8.9 fusion.229
  1224.6 55.6 %reduce-scatter.10.cloned.1.call-done = bf16[24,48,128]{2,1,0:T(8,128)(2,1)} async-done(((bf16[384,48,128]{2,1,0:T(8,128)(2,1)}), bf16[24,48,128]{2,1,0:T(8,128)(2,1)}) %reduce-scatter.10.cloned.1.call-update) | async-done | bytes 294928 | tf_op jit(solution)/shard_map/while/body/eval_jaxpr/reduce_scatter | solution.py:167
  1296.7 67.2 %reduce-scatter.12.cloned.1.call-done = bf16[24,32]{1,0:T(8,128)(2,1)} async-done(((bf16[384,32]{1,0:T(8,128)(2,1)}), bf16[24,32]{1,0:T(8,128)(2,1)}) %reduce-scatter.12.cloned.1.call-update) | async-done | bytes 1552 | tf_op jit(solution)/shard_map/while
  1371.0 17.2 all_gather.55
  1394.1 58.0 %all-gather.7.cloned.1.call-done = bf16[384,48,128]{2,1,0:T(8,128)(2,1)} async-done(((bf16[24,48,128]{2,1,0:T(8,128)(2,1)}), bf16[384,48,128]{2,1,0:T(8,128)(2,1)}) %all-gather.7.cloned.1.call-update) | async-done | bytes 4718608 | tf_op jit(solution)/shard_map/while/body/eval_jaxpr/all_gather | solution.py:127
  1452.1 17.9 copy.214
  1470.0 10.8 convert_bitcast_fusion.7
  1486.8 29.7 %reduce-scatter.8.cloned.1.call-done = bf16[48,24,128]{2,1,0:T(8,128)(2,1)} async-done(((bf16[384,24,128]{2,1,0:T(8,128)(2,1)}), bf16[48,24,128]{2,1,0:T(8,128)(2,1)}) %reduce-scatter.8.cloned.1.call-update) | async-done | bytes 294928 | tf_op jit(solution)/shard_map/while/body/eval_jaxpr/reduce_scatter | solution.py:129
  1532.4 28.2 %all-gather.9.cloned.1.call-done = bf16[24,384,128]{2,0,1:T(8,128)(2,1)} async-done(((bf16[24,48,128]{2,0,1:T(8,128)(2,1)}), bf16[24,384,128]{2,0,1:T(8,128)(2,1)}) %all-gather.9.cloned.1.call-update) | async-done | bytes 2359312 | tf_op jit(solution)/shard_map/while/body/eval_jaxpr/all_gather | solution.py:165
  1585.0 8.9 fusion.229
  1599.7 55.6 %reduce-scatter.10.cloned.1.call-done = bf16[24,48,128]{2,1,0:T(8,128)(2,1)} async-done(((bf16[384,48,128]{2,1,0:T(8,128)(2,1)}), bf16[24,48,128]{2,1,0:T(8,128)(2,1)}) %reduce-scatter.10.cloned.1.call-update) | async-done | bytes 294928 | tf_op jit(solution)/shard_map/while/body/eval_jaxpr/reduce_scatter | solution.py:167
  1671.7 67.2 %reduce-scatter.12.cloned.1.call-done = bf16[24,32]{1,0:T(8,128)(2,1)} async-done(((bf16[384,32]{1,0:T(8,128)(2,1)}), bf16[24,32]{1,0:T(8,128)(2,1)}) %reduce-scatter.12.cloned.1.call-update) | async-done | bytes 1552 | tf_op jit(solution)/shard_map/while
  1746.4 66.9 %all-reduce.9 = (f32[128,64]{1,0:T(8,128)S(1)}, f32[2,128]{0,1:T(8,128)S(1)}) all-reduce(f32[128,64]{1,0:T(8,128)S(1)} %copy.149, f32[2,128]{0,1:T(8,128)S(1)} %copy.150), channel_id=10, replica_groups=mesh['wide'=16,'narrow'=8] {'wide','narrow'}, use_global_device_ids=true, to_apply=%region_31.32.clone | all-reduce | flops 8448 | bytes 67584
  1814.5 86.3 %all-reduce.13.cloned.1.call-done = (f32[33,1024]{0,1:T(8,128)}, f32[1024,64]{1,0:T(8,128)}, f32[1024,128]{1,0:T(8,128)}, f32[128,640]{1,0:T(8,128)}, f32[128,128]{1,0:T(8,128)}) async-done(((f32[33,1024]{0,1:T(8,128)}, f32[1024,64]{1,0:T(8,128)}, f32[1024,128]{1,0:T(8,128)}, f32[128,640]{1,0:T(8,128)}, f32[128,128]{1,0:T(8,128)}), (f32[33,1024]{0,1:T(8,128)}, f32[1024,64]{1,0:T(8,128)}, ...) | async-done | bytes 1314832
  1911.9 64.5 %all-reduce.8 = (f32[]{:T(128)}, f32[]{:T(128)}) all-reduce(f32[]{:T(128)} %get-tuple-element.420, f32[]{:T(128)S(6)} %add.300), channel_id=1, replica_groups=mesh['wide'=16,'narrow'=8] {'wide','narrow'}, use_global_device_ids=true, to_apply=%region_20.21 | all-reduce | flops 2 | bytes 16 | tf_op jit(solution)/shard_map/psum | solution.py:232
  (745 shorter events, 344.5 us)
Async XLA Ops:
  245.8 81.1 %all-gather.7.cloned.1.call-start = ((), (), s32[]{:S(2)}) async-start(), calls=%async_computation.4 | async-start | bytes 5013504 | tf_op jit(solution)/shard_map/while/body/eval_jaxpr/all_gather | solution.py:127
  270.4 120.8 %reduce-scatter.8.cloned.1.call-start = ((), (), s32[]{:S(2)}) async-start(), calls=%async_computation.5 | async-start | bytes 2654208 | tf_op jit(solution)/shard_map/while/body/eval_jaxpr/reduce_scatter | solution.py:129
  360.2 75.2 %all-gather.9.cloned.1.call-start = ((), (), s32[]{:S(2)}) async-start(), calls=%async_computation.6 | async-start | bytes 2654208 | tf_op jit(solution)/shard_map/while/body/eval_jaxpr/all_gather | solution.py:165
  407.1 123.0 %reduce-scatter.10.cloned.1.call-start = ((), (), s32[]{:S(2)}) async-start(), calls=%async_computation.7 | async-start | bytes 5013504 | tf_op jit(solution)/shard_map/while/body/eval_jaxpr/reduce_scatter | solution.py:167
  453.3 160.3 %reduce-scatter.12.cloned.1.call-start = ((), (), s32[]{:S(2)}) async-start(), calls=%async_computation.8 | async-start | bytes 104448 | tf_op jit(solution)/shard_map/while
  542.7 71.6 %copy-start.8 = (f32[1024,64]{1,0:T(8,128)S(1)}, f32[1024,64]{1,0:T(8,128)}, u32[]{:S(2)}) copy-start(f32[1024,64]{1,0:T(8,128)} %get-tuple-element.1010) | copy-start | bytes 786436 | tf_op jit(solution)/shard_map/while
  544.8 71.7 %copy-start.13 = (bf16[1024,64]{1,0:T(8,128)(2,1)S(1)}, bf16[1024,64]{1,0:T(8,128)(2,1)}, u32[]{:S(2)}) copy-start(bf16[1024,64]{1,0:T(8,128)(2,1)} %copy-done.12) | copy-start | bytes 393220 | tf_op jit(solution)/shard_map/while
  616.5 85.5 %all-gather.7.cloned.1.call-start = ((), (), s32[]{:S(2)}) async-start(), calls=%async_computation.4 | async-start | bytes 5013504 | tf_op jit(solution)/shard_map/while/body/eval_jaxpr/all_gather | solution.py:127
  641.7 124.6 %reduce-scatter.8.cloned.1.call-start = ((), (), s32[]{:S(2)}) async-start(), calls=%async_computation.5 | async-start | bytes 2654208 | tf_op jit(solution)/shard_map/while/body/eval_jaxpr/reduce_scatter | solution.py:129
  735.3 75.2 %all-gather.9.cloned.1.call-start = ((), (), s32[]{:S(2)}) async-start(), calls=%async_computation.6 | async-start | bytes 2654208 | tf_op jit(solution)/shard_map/while/body/eval_jaxpr/all_gather | solution.py:165
  782.2 123.0 %reduce-scatter.10.cloned.1.call-start = ((), (), s32[]{:S(2)}) async-start(), calls=%async_computation.7 | async-start | bytes 5013504 | tf_op jit(solution)/shard_map/while/body/eval_jaxpr/reduce_scatter | solution.py:167
  828.4 160.3 %reduce-scatter.12.cloned.1.call-start = ((), (), s32[]{:S(2)}) async-start(), calls=%async_computation.8 | async-start | bytes 104448 | tf_op jit(solution)/shard_map/while
  917.8 71.6 %copy-start.8 = (f32[1024,64]{1,0:T(8,128)S(1)}, f32[1024,64]{1,0:T(8,128)}, u32[]{:S(2)}) copy-start(f32[1024,64]{1,0:T(8,128)} %get-tuple-element.1010) | copy-start | bytes 786436 | tf_op jit(solution)/shard_map/while
  919.9 71.7 %copy-start.13 = (bf16[1024,64]{1,0:T(8,128)(2,1)S(1)}, bf16[1024,64]{1,0:T(8,128)(2,1)}, u32[]{:S(2)}) copy-start(bf16[1024,64]{1,0:T(8,128)(2,1)} %copy-done.12) | copy-start | bytes 393220 | tf_op jit(solution)/shard_map/while
  991.6 85.5 %all-gather.7.cloned.1.call-start = ((), (), s32[]{:S(2)}) async-start(), calls=%async_computation.4 | async-start | bytes 5013504 | tf_op jit(solution)/shard_map/while/body/eval_jaxpr/all_gather | solution.py:127
  1016.8 124.6 %reduce-scatter.8.cloned.1.call-start = ((), (), s32[]{:S(2)}) async-start(), calls=%async_computation.5 | async-start | bytes 2654208 | tf_op jit(solution)/shard_map/while/body/eval_jaxpr/reduce_scatter | solution.py:129
  1110.3 75.2 %all-gather.9.cloned.1.call-start = ((), (), s32[]{:S(2)}) async-start(), calls=%async_computation.6 | async-start | bytes 2654208 | tf_op jit(solution)/shard_map/while/body/eval_jaxpr/all_gather | solution.py:165
  1157.3 123.0 %reduce-scatter.10.cloned.1.call-start = ((), (), s32[]{:S(2)}) async-start(), calls=%async_computation.7 | async-start | bytes 5013504 | tf_op jit(solution)/shard_map/while/body/eval_jaxpr/reduce_scatter | solution.py:167
  1203.5 160.3 %reduce-scatter.12.cloned.1.call-start = ((), (), s32[]{:S(2)}) async-start(), calls=%async_computation.8 | async-start | bytes 104448 | tf_op jit(solution)/shard_map/while
  1295.0 71.7 %copy-start.13 = (bf16[1024,64]{1,0:T(8,128)(2,1)S(1)}, bf16[1024,64]{1,0:T(8,128)(2,1)}, u32[]{:S(2)}) copy-start(bf16[1024,64]{1,0:T(8,128)(2,1)} %copy-done.12) | copy-start | bytes 393220 | tf_op jit(solution)/shard_map/while
  1366.7 85.5 %all-gather.7.cloned.1.call-start = ((), (), s32[]{:S(2)}) async-start(), calls=%async_computation.4 | async-start | bytes 5013504 | tf_op jit(solution)/shard_map/while/body/eval_jaxpr/all_gather | solution.py:127
  1391.9 124.6 %reduce-scatter.8.cloned.1.call-start = ((), (), s32[]{:S(2)}) async-start(), calls=%async_computation.5 | async-start | bytes 2654208 | tf_op jit(solution)/shard_map/while/body/eval_jaxpr/reduce_scatter | solution.py:129
  1485.4 75.2 %all-gather.9.cloned.1.call-start = ((), (), s32[]{:S(2)}) async-start(), calls=%async_computation.6 | async-start | bytes 2654208 | tf_op jit(solution)/shard_map/while/body/eval_jaxpr/all_gather | solution.py:165
  1532.3 123.0 %reduce-scatter.10.cloned.1.call-start = ((), (), s32[]{:S(2)}) async-start(), calls=%async_computation.7 | async-start | bytes 5013504 | tf_op jit(solution)/shard_map/while/body/eval_jaxpr/reduce_scatter | solution.py:167
  1578.6 160.3 %reduce-scatter.12.cloned.1.call-start = ((), (), s32[]{:S(2)}) async-start(), calls=%async_computation.8 | async-start | bytes 104448 | tf_op jit(solution)/shard_map/while
  1670.0 71.7 %copy-start.13 = (bf16[1024,64]{1,0:T(8,128)(2,1)S(1)}, bf16[1024,64]{1,0:T(8,128)(2,1)}, u32[]{:S(2)}) copy-start(bf16[1024,64]{1,0:T(8,128)(2,1)} %copy-done.12) | copy-start | bytes 393220 | tf_op jit(solution)/shard_map/while
  1741.9 235.2 %copy-start.48 = (f32[8,128]{1,0:T(8,128)S(1)}, f32[8,128]{1,0:T(8,128)}, u32[]{:S(2)}) copy-start(f32[8,128]{1,0:T(8,128)} %param.31) | copy-start | bytes 12292
  1741.9 235.2 %copy-start.52 = (f32[8,128]{1,0:T(8,128)S(1)}, f32[8,128]{1,0:T(8,128)}, u32[]{:S(2)}) copy-start(f32[8,128]{1,0:T(8,128)} %param.38) | copy-start | bytes 12292
  1741.9 235.2 %copy-start.53 = (f32[8,128]{1,0:T(8,128)S(1)}, f32[8,128]{1,0:T(8,128)}, u32[]{:S(2)}) copy-start(f32[8,128]{1,0:T(8,128)} %param.45) | copy-start | bytes 12292
  1741.9 236.5 %copy-start.49 = (f32[8,64]{1,0:T(8,128)S(1)}, f32[8,64]{1,0:T(8,128)}, u32[]{:S(2)}) copy-start(f32[8,64]{1,0:T(8,128)} %param.30) | copy-start | bytes 6148
  1741.9 236.5 %copy-start.54 = (f32[8,64]{1,0:T(8,128)S(1)}, f32[8,64]{1,0:T(8,128)}, u32[]{:S(2)}) copy-start(f32[8,64]{1,0:T(8,128)} %param.37) | copy-start | bytes 6148
  1741.9 236.5 %copy-start.55 = (f32[8,64]{1,0:T(8,128)S(1)}, f32[8,64]{1,0:T(8,128)}, u32[]{:S(2)}) copy-start(f32[8,64]{1,0:T(8,128)} %param.44) | copy-start | bytes 6148
  1742.0 237.8 %copy-start.50 = (f32[33,8]{0,1:T(8,128)S(1)}, f32[33,8]{0,1:T(8,128)}, u32[]{:S(2)}) copy-start(f32[33,8]{0,1:T(8,128)} %param.29) | copy-start | bytes 3172
  1742.0 237.8 %copy-start.56 = (f32[33,8]{0,1:T(8,128)S(1)}, f32[33,8]{0,1:T(8,128)}, u32[]{:S(2)}) copy-start(f32[33,8]{0,1:T(8,128)} %param.36) | copy-start | bytes 3172
  1742.0 237.8 %copy-start.57 = (f32[33,8]{0,1:T(8,128)S(1)}, f32[33,8]{0,1:T(8,128)}, u32[]{:S(2)}) copy-start(f32[33,8]{0,1:T(8,128)} %param.43) | copy-start | bytes 3172
  1742.0 239.1 %copy-start.51 = (f32[1,640]{1,0:T(1,128)S(1)}, f32[1,640]{1,0:T(1,128)}, u32[]{:S(2)}) copy-start(f32[1,640]{1,0:T(1,128)} %param.32) | copy-start | bytes 7684
  1742.0 239.1 %copy-start.58 = (f32[1,640]{1,0:T(1,128)S(1)}, f32[1,640]{1,0:T(1,128)}, u32[]{:S(2)}) copy-start(f32[1,640]{1,0:T(1,128)} %param.39) | copy-start | bytes 7684
  1742.0 239.1 %copy-start.59 = (f32[1,640]{1,0:T(1,128)S(1)}, f32[1,640]{1,0:T(1,128)}, u32[]{:S(2)}) copy-start(f32[1,640]{1,0:T(1,128)} %param.46) | copy-start | bytes 7684
  1742.0 240.4 %copy-start.60 = (f32[2,1]{0,1:T(1,128)S(1)}, f32[2,1]{0,1:T(1,128)}, u32[]{:S(2)}) copy-start(f32[2,1]{0,1:T(1,128)} %param.35) | copy-start | bytes 28
  1742.0 240.4 %copy-start.61 = (f32[2,1]{0,1:T(1,128)S(1)}, f32[2,1]{0,1:T(1,128)}, u32[]{:S(2)}) copy-start(f32[2,1]{0,1:T(1,128)} %param.42) | copy-start | bytes 28
  1742.1 240.4 %copy-start.62 = (f32[2,1]{0,1:T(1,128)S(1)}, f32[2,1]{0,1:T(1,128)}, u32[]{:S(2)}) copy-start(f32[2,1]{0,1:T(1,128)} %param.49) | copy-start | bytes 28
  1742.1 240.9 %copy-start.63 = (f32[1,64]{1,0:T(1,128)S(1)}, f32[1,64]{1,0:T(1,128)}, u32[]{:S(2)}) copy-start(f32[1,64]{1,0:T(1,128)} %param.34) | copy-start | bytes 772
  1742.1 240.9 %copy-start.64 = (f32[1,64]{1,0:T(1,128)S(1)}, f32[1,64]{1,0:T(1,128)}, u32[]{:S(2)}) copy-start(f32[1,64]{1,0:T(1,128)} %param.41) | copy-start | bytes 772
  1742.1 240.9 %copy-start.65 = (f32[1,64]{1,0:T(1,128)S(1)}, f32[1,64]{1,0:T(1,128)}, u32[]{:S(2)}) copy-start(f32[1,64]{1,0:T(1,128)} %param.48) | copy-start | bytes 772
  1742.1 241.5 %copy-start.66 = (f32[1,128]{1,0:T(1,128)S(1)}, f32[1,128]{1,0:T(1,128)}, u32[]{:S(2)}) copy-start(f32[1,128]{1,0:T(1,128)} %param.33) | copy-start | bytes 1540
  1742.1 241.4 %copy-start.67 = (f32[1,128]{1,0:T(1,128)S(1)}, f32[1,128]{1,0:T(1,128)}, u32[]{:S(2)}) copy-start(f32[1,128]{1,0:T(1,128)} %param.40) | copy-start | bytes 1540
  1742.1 241.4 %copy-start.68 = (f32[1,128]{1,0:T(1,128)S(1)}, f32[1,128]{1,0:T(1,128)}, u32[]{:S(2)}) copy-start(f32[1,128]{1,0:T(1,128)} %param.47) | copy-start | bytes 1540
  1742.1 158.7 %all-reduce.13.cloned.1.call-start = ((), (), s32[]{:S(2)}) async-start(), calls=%async_computation.3 | async-start | bytes 3932160
  (184 other events, 3179.4 us)
Sparse Core Ops, SparseCore 0:
  270.5 56.3 all-gather.6
  360.3 30.9 reduce-scatter.7
  407.2 28.1 all-gather.8
  453.4 76.5 reduce-scatter.9
  543.5 70.0 reduce-scatter.11
  641.8 60.0 all-gather.6
  735.4 30.9 reduce-scatter.7
  782.3 28.1 all-gather.8
  828.5 76.5 reduce-scatter.9
  918.6 70.0 reduce-scatter.11
  1016.9 60.0 all-gather.6
  1110.5 30.9 reduce-scatter.7
  1157.4 28.1 all-gather.8
  1203.6 76.5 reduce-scatter.9
  1293.7 70.0 reduce-scatter.11
  1392.0 60.0 all-gather.6
  1485.5 30.9 reduce-scatter.7
  1532.5 28.1 all-gather.8
  1578.7 76.5 reduce-scatter.9
  1668.8 70.0 reduce-scatter.11
Sparse Core Ops, SparseCore 1:
  1748.3 152.5 all-reduce.12
where the time goes:
time: 2000 us; the launch traced here: 1990 us
  waiting for transfers between devices  1040 us (52%)
  blocking collectives  426 us (21%)
  local copies, waits for them, and re-layouts  198 us (10%)
  matrix products  188 us (9%)
  other arithmetic  115 us (6%)
  between operations  22.3 us (1%)
    while x24, waiting for transfers between devices  269 us
    all_gather x4, waiting for transfers between devices, crop_step(): panel = lax.all_gather(right_edge, 'wide', axis=0, tiled=True)  228 us
    reduce_scatter x4, waiting for transfers between devices, crop_step(): lax.psum_scatter(grad_panel.astype(jnp.bfloat16), 'wide', scatter_dimensi...  222 us
    reduce_scatter x4, waiting for transfers between devices, crop_step(): lax.psum_scatter(jnp.einsum('jkc,ikc->jic', piece, left_edge, preferred_e...  119 us
    all_gather x4, waiting for transfers between devices, crop_step(): lax.all_gather(grad_product.astype(bf16), 'narrow', axis=1, tiled=True)  113 us
    unnamed x2, waiting for transfers between devices  86.4 us
    all_gather x4, local copies, waits for them, and re-layouts, crop_step(): panel = lax.all_gather(right_edge, 'wide', axis=0, tiled=True)  71.4 us
    all_gather x4, blocking collectives, crop_step(): lax.all_gather(ab_rows[:, outer_width:], 'wide', axis=0, tiled=True)  68 us
  transfers between devices with their start and end apart: 21, of which 21 were waited for; matrix products, arithmetic and copies ran while one was open for 5% of the time, Pallas kernels for 0%

commit v1 on v0

v1 whole, which is shorter than its diff:
```python
import functools

import jax
import jax.numpy as jnp
from jax import lax
from jax.experimental import pallas as pl
from jax.experimental.pallas import tpu as pltpu
from jax.sharding import PartitionSpec as P

norm_eps = 1e-05
clip_level = 0.001
beta_one = 0.9
beta_two = 0.999
adam_eps = 1e-10
decay_rate = 0.01
step_count = 10.0
rates = (0.5, 0.016, 0.016, 0.044, 0.044, 0.044, 0.5)

f32 = jnp.float32
bf16 = jnp.bfloat16
MESH = pl.DeviceIdType.MESH
VMEM = pltpu.VMEM
LIMIT = 56 * 1024 * 1024

vocab = 33
tokens_padded = 40
table = tokens_padded * tokens_padded
own_rows = 12
bins = 64
narrow_size = 8
wide_size = 16
length = 384


def dot(a, b, axis_a, axis_b, precision=None):
    return lax.dot_general(
        a, b, (((axis_a,), (axis_b,)), ((), ())), precision=precision, preferred_element_type=f32
    )


def rounded(values):
    return values.astype(bf16).astype(f32)


def greet(wide, narrow):
    barrier = pltpu.get_barrier_semaphore()
    for k in range(1, narrow_size):
        peer = lax.rem(narrow + k, narrow_size)
        pl.semaphore_signal(barrier, inc=1, device_id=(wide, peer), device_id_type=MESH)
    for k in range(1, wide_size):
        peer = lax.rem(wide + k, wide_size)
        pl.semaphore_signal(barrier, inc=1, device_id=(peer, narrow), device_id_type=MESH)
    pl.semaphore_wait(barrier, narrow_size + wide_size - 2)


def gather_kernel(
    tgt, emb, ab, outer, tri, mix, dist, gain,
    g_out, t_out, tgt_out,
    pack, tstage, stage, taken, part, taken_t, source, source_t, taken_w,
    send_a, recv_a, send_t, recv_t, send_b, recv_b, send_u, recv_u,
):
    wide = lax.axis_index("wide")
    narrow = lax.axis_index("narrow")
    greet(wide, narrow)
    pack[...] = jnp.zeros_like(pack)
    pack[0:8, :] = outer[...]
    for m in range(5):
        pack[8 + m : 9 + m, :] = tri[:, 128 * m : 128 * m + 128]
    pack[13:14, :] = mix[...]
    pack[14:15, 0:64] = dist[...]
    pack[14:15, 64:66] = gain[...]
    low = pack[...].astype(bf16)
    tstage[...] = jnp.zeros_like(tstage)
    for m in range(narrow_size):
        start = 8 * (m % 2)
        tstage[m, :, 0:48] = tgt[m // 2, start : start + 16, :].astype(f32)
        stage[m, 0:16, :] = low
        stage[m, 16:32, :] = tstage[m].astype(bf16)
    part[...] = jnp.zeros_like(part)
    part[0:vocab, 0:64] = dot(emb[...].astype(bf16), ab[...].astype(bf16), 0, 0)

    copies = []
    for k in range(1, narrow_size):
        peer = lax.rem(narrow + k, narrow_size)
        copies.append(
            pltpu.make_async_remote_copy(
                src_ref=stage.at[peer], dst_ref=taken.at[narrow],
                send_sem=send_a.at[k], recv_sem=recv_a.at[k],
                device_id=(wide, peer), device_id_type=MESH,
            )
        )
        copies.append(
            pltpu.make_async_remote_copy(
                src_ref=part, dst_ref=taken_t.at[narrow],
                send_sem=send_t.at[k], recv_sem=recv_t.at[k],
                device_id=(wide, peer), device_id_type=MESH,
            )
        )
    for copy in copies:
        copy.start()
    taken[narrow] = stage[narrow]
    taken_t[narrow] = part[...]
    for copy in copies:
        copy.wait()
    total = taken_t[0]
    for m in range(1, narrow_size):
        total = total + taken_t[m]
    source_t[...] = total
    for m in range(narrow_size):
        source[16 * m : 16 * m + 16, :] = taken[m, 0:16, :]
        tgt_out[m] = taken[m, 16:32, :]

    place = pl.ds(pl.multiple_of(wide * 128, 128), 128)
    copies = []
    for k in range(1, wide_size):
        peer = lax.rem(wide + k, wide_size)
        copies.append(
            pltpu.make_async_remote_copy(
                src_ref=source_t, dst_ref=taken_w.at[wide],
                send_sem=send_u.at[k], recv_sem=recv_u.at[k],
                device_id=(peer, narrow), device_id_type=MESH,
            )
        )
        copies.append(
            pltpu.make_async_remote_copy(
                src_ref=source, dst_ref=g_out.at[place],
                send_sem=send_b.at[k], recv_sem=recv_b.at[k],
                device_id=(peer, narrow), device_id_type=MESH,
            )
        )
    for copy in copies:
        copy.start()
    g_out[place, :] = source[...]
    taken_w[wide] = source_t[...]
    for copy in copies:
        copy.wait()
    total = taken_w[0]
    for m in range(1, wide_size):
        total = total + taken_w[m]
    t_out[...] = total


def class_kernel(
    tok_s, seg_s, tok_v, seg_v, tgt, gathered, factors,
    grads_out, d_out,
    weights, tg, u, z, xhat, rstd, zn, sa, pa, sb, pb, ta, tb, sgo,
    hist, many, wa, zi, so, x, dx, dgo, dz1, ga, gb, go, gz, dp, dz, du, grads,
):
    wide = lax.axis_index("wide")
    narrow = lax.axis_index("narrow")
    crop = narrow // 2
    half = lax.rem(narrow, 2)
    row0 = wide * 24 + half * own_rows
    rows = tokens_padded

    weights[...] = gathered[...].astype(f32)
    factor = factors[...].astype(bf16)
    a = factor[:, 0:32]
    b = factor[:, 32:64]
    w_outer = jnp.concatenate(
        [weights[pl.ds(16 * (q // 8) + q % 8, 32, stride=64), :] for q in range(32)], axis=1
    ).astype(bf16)
    w_tri = jnp.concatenate(
        [weights[pl.ds(8 + m, 128, stride=16), :] for m in range(5)], axis=1
    ).astype(bf16)
    w_mix = weights[pl.ds(13, 128, stride=16), :].astype(bf16)
    tail_t = weights[pl.ds(14, 128, stride=16), :].T
    dist_t = tail_t[0:bins, :].astype(bf16)
    gain_in = tail_t[64:65, :]
    gain_mid = tail_t[65:66, :]

    u_q = rounded(dot(a, w_outer, 1, 0))
    for q in range(32):
        u[pl.ds(q, rows, stride=32), :] = u_q[:, 128 * q : 128 * q + 128]
    u_cat = jnp.concatenate([u[32 * t : 32 * t + 32, :] for t in range(rows)], axis=1).astype(bf16)
    z_cat = dot(b, u_cat, 1, 0)
    for t in range(rows):
        z[rows * t : rows * t + rows, :] = z_cat[:, 128 * t : 128 * t + 128]

    chunk = 160

    def forward(step, carry):
        at = pl.ds(pl.multiple_of(step * chunk, chunk), chunk)
        values = z[at, :]
        center = values - jnp.mean(values, -1, keepdims=True)
        inverse = lax.rsqrt(jnp.mean(center * center, -1, keepdims=True) + norm_eps)
        scaled = center * inverse
        normed = (scaled * gain_in).astype(bf16)
        xhat[at, :] = scaled
        rstd[at, :] = jnp.broadcast_to(inverse, scaled.shape)
        zn[at, :] = normed
        projected = dot(normed, w_tri, 1, 0)
        gate = jax.nn.sigmoid(projected[:, 0:128])
        value = projected[:, 128:256]
        sa[at, :] = gate
        pa[at, :] = value
        ta[at, :] = rounded(gate * value)
        gate = jax.nn.sigmoid(projected[:, 256:384])
        value = projected[:, 384:512]
        sb[at, :] = gate
        pb[at, :] = value
        tb[at, :] = rounded(gate * value)
        sgo[at, :] = jax.nn.sigmoid(projected[:, 512:640])
        return carry

    lax.fori_loop(0, table // chunk, forward, 0)

    count = jnp.zeros((4, 1), f32)
    for s in range(6):
        members = jnp.sum((seg_v[...] == s).astype(f32), axis=1, keepdims=True)
        count = count + members * members
    count = jnp.sum(count, axis=0, keepdims=True)

    for m in range(narrow_size):
        tg[:, 48 * m : 48 * m + 48] = tgt[m].astype(f32)[:, 0:48]
    tok_row = tok_v[pl.ds(crop, 1), :]
    seg_row = seg_v[pl.ds(crop, 1), :]
    hot = (lax.broadcasted_iota(jnp.int32, (rows, length), 0) == tok_row).astype(f32).astype(bf16)
    bin_of = lax.broadcasted_iota(jnp.int32, (bins, length), 0).astype(f32)
    starts = []
    for i in range(own_rows):
        kind = tok_s[crop, row0 + i]
        start = pl.ds(pl.multiple_of(kind * rows, 8), rows)
        starts.append(start)
        here = slice(rows * i, rows * i + rows)
        wanted = jnp.where(seg_row == seg_s[crop, row0 + i], tg[pl.ds(4 * half + i, 1), :], -1.0)
        counts = dot(hot, (bin_of == wanted).astype(f32).astype(bf16), 1, 1)
        number = jnp.sum(counts, -1, keepdims=True)
        hist[here, :] = counts
        many[here, :] = jnp.broadcast_to(number, (rows, 128))
        wa[here, :] = number * ta[start, :]
        zi[here, :] = z[start, :]
        so[here, :] = sgo[start, :]

    for group in range(own_rows // 4):
        own = range(4 * group, 4 * group + 4)

        def product(v, sums, own=own):
            edge = tb[pl.ds(v, rows, stride=rows), :]
            return tuple(
                total + wa[pl.ds(rows * i + v, 1), :] * edge for total, i in zip(sums, own)
            )

        sums = lax.fori_loop(0, vocab, product, (jnp.zeros((rows, 128), f32),) * 4)
        for total, i in zip(sums, own):
            x[rows * i : rows * i + rows, :] = total

    values = x[...]
    center = values - jnp.mean(values, -1, keepdims=True)
    inverse = lax.rsqrt(jnp.mean(center * center, -1, keepdims=True) + norm_eps)
    scaled = center * inverse
    mixed = (scaled * gain_mid).astype(bf16)
    branch = dot(mixed, w_mix, 1, 0)
    gate_out = so[...]
    update = (zi[...] + gate_out * branch).astype(bf16)
    logits = dot(update, dist_t, 1, 1)
    top = jnp.max(logits, -1, keepdims=True)
    powers = jnp.exp(logits - top)
    power_sum = jnp.sum(powers, -1, keepdims=True)
    counts = hist[...]
    number = many[:, 0:bins]
    loss = jnp.sum(many[:, 0:1] * (jnp.log(power_sum) + top), axis=0, keepdims=True) - jnp.sum(
        jnp.sum(counts * logits, axis=1, keepdims=True), axis=0, keepdims=True
    )
    grad_logits = ((number * (powers / power_sum) - counts) / count).astype(bf16)
    grad_dist_t = dot(grad_logits, update, 0, 0)
    grad_update = dot(grad_logits, dist_t, 1, 0)
    grad_branch = (grad_update * gate_out).astype(bf16)
    dz1[...] = grad_update
    dgo[...] = grad_update * branch * gate_out * (1.0 - gate_out)
    grad_mix = dot(mixed, grad_branch, 0, 0)
    grad_mixed = dot(grad_branch, w_mix, 1, 1)
    grad_gain_mid = jnp.sum(grad_mixed * scaled, axis=0, keepdims=True)
    grad_hat = grad_mixed * gain_mid
    dx[...] = inverse * (
        grad_hat
        - jnp.mean(grad_hat, -1, keepdims=True)
        - scaled * jnp.mean(grad_hat * scaled, -1, keepdims=True)
    )

    for ref in (ga, gb, go, gz):
        ref[...] = jnp.zeros_like(ref)
    for group in range(own_rows // 4):
        own = range(4 * group, 4 * group + 4)
        weighted = [wa[rows * i : rows * i + rows, :] for i in own]

        def edges(t, sums, own=own, weighted=weighted):
            at = pl.ds(pl.multiple_of(t * rows, 8), rows)
            edge = tb[at, :]
            right = gb[at, :]
            news = []
            for total, i, left in zip(sums, own, weighted):
                grad = dx[pl.ds(rows * i + t, 1), :]
                news.append(total + grad * edge)
                right = right + grad * left
            gb[at, :] = right
            return tuple(news)

        sums = lax.fori_loop(0, vocab, edges, (jnp.zeros((rows, 128), f32),) * 4)
        for total, i in zip(sums, own):
            here = slice(rows * i, rows * i + rows)
            ga[starts[i], :] += total * many[here, :]
            go[starts[i], :] += dgo[here, :]
            gz[starts[i], :] += dz1[here, :]

    def backward(step, grad_gain):
        at = pl.ds(pl.multiple_of(step * chunk, chunk), chunk)
        gate = sa[at, :]
        grad = ga[at, :] * gate
        dp[at, 0:128] = (grad * pa[at, :] * (1.0 - gate)).astype(bf16)
        dp[at, 128:256] = grad.astype(bf16)
        gate = sb[at, :]
        grad = gb[at, :] * gate
        dp[at, 256:384] = (grad * pb[at, :] * (1.0 - gate)).astype(bf16)
        dp[at, 384:512] = grad.astype(bf16)
        dp[at, 512:640] = go[at, :].astype(bf16)
        grad_normed = dot(dp[at, :], w_tri, 1, 1)
        scaled = xhat[at, :]
        grad_gain = grad_gain + jnp.sum(grad_normed * scaled, axis=0, keepdims=True)
        grad_hat = grad_normed * gain_in
        dz[at, :] = gz[at, :] + rstd[at, :] * (
            grad_hat
            - jnp.mean(grad_hat, -1, keepdims=True)
            - scaled * jnp.mean(grad_hat * scaled, -1, keepdims=True)
        )
        return grad_gain

    grad_gain_in = lax.fori_loop(0, table // chunk, backward, jnp.zeros((1, 128), f32))
    grad_tri = dot(zn[...], dp[...], 0, 0)

    def parts(values):
        high = values.astype(bf16)
        return high, (values - high.astype(f32)).astype(bf16)

    dz_high, dz_low = parts(
        jnp.concatenate([dz[rows * t : rows * t + rows, :] for t in range(rows)], axis=1)
    )
    grad_u = dot(b, dz_high, 0, 0) + dot(b, dz_low, 0, 0)
    for t in range(rows):
        du[32 * t : 32 * t + 32, :] = grad_u[:, 128 * t : 128 * t + 128]
    grad_b = dot(dz_high, u_cat, 1, 1) + dot(dz_low, u_cat, 1, 1)
    du_high, du_low = parts(
        jnp.concatenate([du[pl.ds(q, rows, stride=32), :] for q in range(32)], axis=1)
    )
    grad_outer = dot(a, du_high, 0, 0) + dot(a, du_low, 0, 0)
    grad_a = dot(du_high, w_outer, 1, 1) + dot(du_low, w_outer, 1, 1)

    grads[...] = jnp.zeros_like(grads)
    for q in range(32):
        grads[pl.ds(16 * (q // 8) + q % 8, 32, stride=64), :] = grad_outer[:, 128 * q : 128 * q + 128]
    for m in range(5):
        grads[pl.ds(8 + m, 128, stride=16), :] = grad_tri[:, 128 * m : 128 * m + 128]
    grads[pl.ds(13, 128, stride=16), :] = grad_mix
    grads[pl.ds(14, 128, stride=16), :] = jnp.concatenate(
        [grad_dist_t, grad_gain_in, grad_gain_mid, jnp.zeros((62, 128), f32)], axis=0
    ).T
    grads_out[...] = grads[...].astype(bf16)
    line = lax.broadcasted_iota(jnp.int32, (rows, 128), 0)
    lane = lax.broadcasted_iota(jnp.int32, (rows, 128), 1)
    d_out[...] = jnp.where((line == 0) & (lane == 64), loss, 0.0)
    d_out[:, 0:32] = grad_a
    d_out[:, 32:64] = grad_b


def reduce_kernel(
    grads, factor_grads, emb, ab,
    out,
    taken, taken_d, total_g, total_d, taken_n, taken_e, square, square_n, square_w,
    send_a, recv_a, send_d, recv_d, send_b, recv_b, send_e, recv_e, send_m, recv_m, send_w, recv_w,
):
    wide = lax.axis_index("wide")
    narrow = lax.axis_index("narrow")
    greet(wide, narrow)

    copies = []
    for k in range(1, wide_size):
        peer = lax.rem(wide + k, wide_size)
        copies.append(
            pltpu.make_async_remote_copy(
                src_ref=grads.at[pl.ds(pl.multiple_of(peer * 128, 128), 128)], dst_ref=taken.at[wide],
                send_sem=send_a.at[k], recv_sem=recv_a.at[k],
                device_id=(peer, narrow), device_id_type=MESH,
            )
        )
        copies.append(
            pltpu.make_async_remote_copy(
                src_ref=factor_grads, dst_ref=taken_d.at[wide],
                send_sem=send_d.at[k], recv_sem=recv_d.at[k],
                device_id=(peer, narrow), device_id_type=MESH,
            )
        )
    for copy in copies:
        copy.start()
    taken[wide] = grads[pl.ds(pl.multiple_of(wide * 128, 128), 128), :]
    taken_d[wide] = factor_grads[...]
    for copy in copies:
        copy.wait()
    total = taken[0].astype(f32)
    small = taken_d[0]
    for m in range(1, wide_size):
        total = total + taken[m].astype(f32)
        small = small + taken_d[m]
    total_g[...] = total
    total_d[...] = small

    copies = []
    for k in range(1, narrow_size):
        peer = lax.rem(narrow + k, narrow_size)
        copies.append(
            pltpu.make_async_remote_copy(
                src_ref=total_g.at[pl.ds(pl.multiple_of(peer * 16, 16), 16)], dst_ref=taken_n.at[narrow],
                send_sem=send_b.at[k], recv_sem=recv_b.at[k],
                device_id=(wide, peer), device_id_type=MESH,
            )
        )
        copies.append(
            pltpu.make_async_remote_copy(
                src_ref=total_d, dst_ref=taken_e.at[narrow],
                send_sem=send_e.at[k], recv_sem=recv_e.at[k],
                device_id=(wide, peer), device_id_type=MESH,
            )
        )
    for copy in copies:
        copy.start()
    taken_n[narrow] = total_g[pl.ds(pl.multiple_of(narrow * 16, 16), 16), :]
    taken_e[narrow] = total_d[...]
    for copy in copies:
        copy.wait()
    total = taken_n[0]
    small = taken_e[0]
    for m in range(1, narrow_size):
        total = total + taken_n[m]
        small = small + taken_e[m]

    highest = lax.Precision.HIGHEST
    factor_grad = small[:, 0:64]
    grad_emb = dot(rounded(ab[...]), factor_grad, 1, 1, highest)
    grad_ab = dot(rounded(emb[...]), factor_grad[0:vocab, :], 1, 0, highest)
    out[0:16, :] = total
    out[16:24, :] = jnp.zeros((8, 128), f32)
    out[24:32, :] = jnp.zeros((8, 128), f32)
    out[16:24, 0:tokens_padded] = grad_emb
    out[24:32, 0:64] = grad_ab
    squares = jnp.sum(jnp.sum(total * total, axis=1, keepdims=True), axis=0, keepdims=True)
    squares += jnp.sum(jnp.sum(grad_emb * grad_emb, axis=1, keepdims=True), axis=0, keepdims=True)
    squares += jnp.sum(jnp.sum(grad_ab * grad_ab, axis=1, keepdims=True), axis=0, keepdims=True)
    square[...] = jnp.broadcast_to(squares, square.shape)
    out[40:48, :] = jnp.broadcast_to(small[0:1, 64:65], (8, 128))

    copies = []
    for k in range(1, narrow_size):
        peer = lax.rem(narrow + k, narrow_size)
        copies.append(
            pltpu.make_async_remote_copy(
                src_ref=square, dst_ref=square_n.at[narrow],
                send_sem=send_m.at[k], recv_sem=recv_m.at[k],
                device_id=(wide, peer), device_id_type=MESH,
            )
        )
    for copy in copies:
        copy.start()
    square_n[narrow] = square[...]
    for copy in copies:
        copy.wait()
    total = square_n[0]
    for m in range(1, narrow_size):
        total = total + square_n[m]
    square[...] = total
    copies = []
    for k in range(1, wide_size):
        peer = lax.rem(wide + k, wide_size)
        copies.append(
            pltpu.make_async_remote_copy(
                src_ref=square, dst_ref=square_w.at[wide],
                send_sem=send_w.at[k], recv_sem=recv_w.at[k],
                device_id=(peer, narrow), device_id_type=MESH,
            )
        )
    for copy in copies:
        copy.start()
    square_w[wide] = square[...]
    for copy in copies:
        copy.wait()
    total = square_w[0]
    for m in range(1, wide_size):
        total = total + square_w[m]
    out[32:40, :] = total


def update_kernel(seg_v, reduced, *refs):
    weights, firsts, seconds = refs[0:7], refs[7:14], refs[14:21]
    loss_out, count_out, norm_out = refs[21:24]
    news, moms, vels = refs[24:31], refs[31:38], refs[38:45]
    count = jnp.zeros((4, 1), f32)
    for s in range(6):
        members = jnp.sum((seg_v[...] == s).astype(f32), axis=1, keepdims=True)
        count = count + members * members
    count_out[...] = jnp.sum(count, axis=0, keepdims=True)
    norm = jnp.sqrt(reduced[32:33, 0:1])
    norm_out[...] = norm
    loss_out[...] = reduced[40:41, 0:1]
    scale = jnp.minimum(1.0, clip_level / norm)
    tri = jnp.concatenate([reduced[8 + m : 9 + m, :] for m in range(5)], axis=1)
    grads = (
        reduced[16:24, 0:vocab],
        reduced[24:32, 0:64],
        reduced[0:8, :],
        tri,
        reduced[13:14, :],
        reduced[14:15, 0:64],
        reduced[14:15, 64:66],
    )
    for at, rate in enumerate(rates):
        clipped = grads[at] * scale
        weight = weights[at][...]
        first = beta_one * firsts[at][...] + (1.0 - beta_one) * clipped
        second = beta_two * seconds[at][...] + (1.0 - beta_two) * clipped * clipped
        ratio = (
            first
            / (1.0 - beta_one**step_count)
            / (jnp.sqrt(second / (1.0 - beta_two**step_count)) + adam_eps)
        )
        news[at][...] = weight - rate * (ratio + decay_rate * weight)
        moms[at][...] = first
        vels[at][...] = second


def shape(*dims, dtype=f32):
    return jax.ShapeDtypeStruct(dims, dtype)


in_vmem = pl.BlockSpec(memory_space=pltpu.VMEM)
in_smem = pl.BlockSpec(memory_space=pltpu.SMEM)


def gather_call(*args):
    dma = pltpu.SemaphoreType.DMA
    return pl.pallas_call(
        gather_kernel,
        out_shape=(
            shape(2048, 128, dtype=bf16),
            shape(tokens_padded, 128),
            shape(narrow_size, 16, 128, dtype=bf16),
        ),
        in_specs=[in_vmem] * len(args),
        out_specs=(in_vmem,) * 3,
        scratch_shapes=[
            VMEM((16, 128), f32),
            VMEM((narrow_size, 16, 128), f32),
            VMEM((narrow_size, 32, 128), bf16),
            VMEM((narrow_size, 32, 128), bf16),
            VMEM((tokens_padded, 128), f32),
            VMEM((narrow_size, tokens_padded, 128), f32),
            VMEM((128, 128), bf16),
            VMEM((tokens_padded, 128), f32),
            VMEM((wide_size, tokens_padded, 128), f32),
            dma((narrow_size,)), dma((narrow_size,)), dma((narrow_size,)), dma((narrow_size,)),
            dma((wide_size,)), dma((wide_size,)), dma((wide_size,)), dma((wide_size,)),
        ],
        compiler_params=pltpu.CompilerParams(
            collective_id=0, has_side_effects=True, vmem_limit_bytes=LIMIT
        ),
        name="gather_weights",
    )(*args)


def class_call(*args):
    wide_table = [VMEM((table, 128), f32)]
    own = [VMEM((own_rows * tokens_padded, 128), f32)]
    return pl.pallas_call(
        class_kernel,
        out_shape=(shape(2048, 128, dtype=bf16), shape(tokens_padded, 128)),
        in_specs=[in_smem] * 2 + [in_vmem] * (len(args) - 2),
        out_specs=(in_vmem,) * 2,
        scratch_shapes=[
            VMEM((2048, 128), f32),
            VMEM((16, length), f32),
            VMEM((32 * tokens_padded, 128), f32),
            *wide_table * 3,
            VMEM((table, 128), bf16),
            *wide_table * 7,
            VMEM((own_rows * tokens_padded, bins), f32),
            *own * 8,
            *wide_table * 4,
            VMEM((table, 640), bf16),
            *wide_table,
            VMEM((32 * tokens_padded, 128), f32),
            VMEM((2048, 128), f32),
        ],
        compiler_params=pltpu.CompilerParams(vmem_limit_bytes=LIMIT),
        name="pair_classes",
    )(*args)


def reduce_call(*args):
    dma = pltpu.SemaphoreType.DMA
    return pl.pallas_call(
        reduce_kernel,
        out_shape=shape(48, 128),
        in_specs=[in_vmem] * len(args),
        out_specs=in_vmem,
        scratch_shapes=[
            VMEM((wide_size, 128, 128), bf16),
            VMEM((wide_size, tokens_padded, 128), f32),
            VMEM((128, 128), f32),
            VMEM((tokens_padded, 128), f32),
            VMEM((narrow_size, 16, 128), f32),
            VMEM((narrow_size, tokens_padded, 128), f32),
            VMEM((8, 128), f32),
            VMEM((narrow_size, 8, 128), f32),
            VMEM((wide_size, 8, 128), f32),
            dma((wide_size,)), dma((wide_size,)), dma((wide_size,)), dma((wide_size,)),
            dma((narrow_size,)), dma((narrow_size,)), dma((narrow_size,)), dma((narrow_size,)),
            dma((narrow_size,)), dma((narrow_size,)), dma((wide_size,)), dma((wide_size,)),
        ],
        compiler_params=pltpu.CompilerParams(
            collective_id=1, has_side_effects=True, vmem_limit_bytes=LIMIT
        ),
        name="reduce_gradients",
    )(*args)


def local(tokens, segments, targets, *state):
    state = list(state)
    for at in (0, 6, 7, 13, 14, 20):
        state[at] = state[at].T
    masters = state[0:7]
    embed, w_ab = masters[0:2]
    gathered, factors, moved = gather_call(targets, *masters)
    grads, factor_grads = class_call(tokens, segments, tokens, segments, moved, gathered, factors)
    reduced = reduce_call(grads, factor_grads, embed, w_ab)
    shapes = [shape(*w.shape) for w in masters]
    outs = pl.pallas_call(
        update_kernel,
        out_shape=[shape(1, 1)] * 3 + shapes * 3,
        in_specs=[in_vmem] * (2 + 21),
        out_specs=[in_vmem] * 24,
        name="update_weights",
    )(segments, reduced, *state)
    outs = [value.reshape(()) for value in outs[0:3]] + list(outs[3:])
    for at in (3, 9, 10, 16, 17, 23):
        outs[at] = outs[at].T
    return tuple(outs)


def solution(mesh):
    both = ("wide", "narrow")
    whole = (P(None, both), P(both, None), P(both, None), P(both, None), P(both, None), P(both, None), P(None, both))
    return jax.shard_map(
        local,
        mesh=mesh,
        in_specs=(P(), P(), P(None, "wide", "narrow")) + whole * 3,
        out_specs=(P(), P(), P()) + whole * 3,
        check_vma=False,
    )
```

time: 2000 us -> 80.9 us (0.04)
  waiting for transfers between devices: 1040 us -> 0 us
  blocking collectives: 426 us -> 0 us
  local copies, waits for them, and re-layouts: 198 us -> 0 us
  matrix products: 188 us -> 0 us
  other arithmetic: 115 us -> 0 us
  Pallas kernels: 0 us -> 80 us
  between operations: 22.3 us -> 0.67 us
    reduce_scatter x8 -> x0, waiting for transfers between devices: 341 us -> none  [the longest x4 222 us: crop_step(): lax.psum_scatter(grad_panel.astype(jnp.bfloat16), 'wide', scatter_dimensi...]
    all_gather x8 -> x0, waiting for transfers between devices: 341 us -> none  [the longest x4 228 us: crop_step(): panel = lax.all_gather(right_edge, 'wide', axis=0, tiled=True)]
    all_gather x11 -> x0, blocking collectives: 294 us -> none  [the longest x4 68 us: crop_step(): lax.all_gather(ab_rows[:, outer_width:], 'wide', axis=0, tiled=True)]
    while x24 -> x0, waiting for transfers between devices: 269 us -> none
    dot_general x88 -> x0, matrix products: 179 us -> none  [the longest x4 43 us: crop_step(): jnp.einsum('jkc,ikc->jic', piece, left_edge, preferred_element_type=f32)]
    all_gather x9 -> x0, local copies, waits for them, and re-layouts: 91.2 us -> none  [the longest x4 71.4 us: crop_step(): panel = lax.all_gather(right_edge, 'wide', axis=0, tiled=True)]
    unnamed x2 -> x0, waiting for transfers between devices: 86.4 us -> none
    pallas_call x0 -> x4, Pallas kernels: none -> 80 us  [the longest x1 32.4 us: reduce_call(): pl.pallas_call(reduce_kernel, out_shape=shape(48, 128), in_specs=[in_vmem...]
  transfers between devices with their start and end apart: 21 -> 0, of which waited for: 21 -> 0; matrix products, arithmetic and copies ran while one was open for 5% -> 0% of each run, Pallas kernels for 0% -> 0%
where the time goes in v1:
time: 80.9 us; the launch traced here: 80.6 us
  Pallas kernels  80 us (99%)
    pallas_call x1, Pallas kernels, reduce_call(): pl.pallas_call(reduce_kernel, out_shape=shape(48, 128), in_specs=[in_vmem...  32.4 us
    pallas_call x1, Pallas kernels, gather_call(): pl.pallas_call(gather_kernel, out_shape=(shape(2048, 128, dtype=bf16), sh...  28.3 us
    pallas_call x1, Pallas kernels, class_call(): pl.pallas_call(class_kernel, out_shape=(shape(2048, 128, dtype=bf16), sha...  17.4 us
    pallas_call x1, Pallas kernels, local(): pl.pallas_call(update_kernel, out_shape=[shape(1, 1)] * 3 + shapes * 3, i...  1.81 us

profile of v1, /device:TPU:1, one launch (start us, length us, event | category | flops | bytes accessed | tf_op | source)
XLA Modules:
  0.0 80.6 jit_solution(14394712464412777430)
XLA Ops:
  0.7 28.3 %gather_weights.1 = (bf16[2048,128]{1,0:T(8,128)(2,1)}, f32[40,128]{1,0:T(8,128)}, bf16[8,16,128]{2,1,0:T(8,128)(2,1)}) custom-call(s32[4,24,48]{2,1,0:T(8,128)} %tgt.1, f32[8,33]{1,0:T(8,128)} %bitcast.15, f32[8,64]{1,0:T(8,128)} %refs_1_.1, f32[8,128]{1,0:T(8,128)} %refs_2_.1, f32[1,640]{1,0:T(1,128)} %refs_3_.1, f32[1,128]{1,0:T(1,128)} %refs_4_.1, ...), custom_call_target="tpu_custom_call" | custom-call | tf_op jit(solution)/shard_map/gather_weights/pallas_call | solution.py:538
  29.0 17.4 %pair_classes.1 = (bf16[2048,128]{1,0:T(8,128)(2,1)}, f32[40,128]{1,0:T(8,128)}) custom-call(s32[4,384]{1,0:T(4,128)} %tok_v.1, s32[4,384]{1,0:T(4,128)} %seg_v.3, s32[4,384]{1,0:T(4,128)} %tok_v.1, s32[4,384]{1,0:T(4,128)} %seg_v.3, bf16[8,16,128]{2,1,0:T(8,128)(2,1)} %get-tuple-element.53.tgt, bf16[2048,128]{1,0:T(8,128)(2,1)} %get-tuple-element.54.gathered, ...), custom_call_target="tpu_custom_call" | custom-call | tf_op jit(solution)/shard_map/pair_classes/pallas_call | solution.py:570
  46.4 32.4 %reduce_gradients.1.reduced = f32[48,128]{1,0:T(8,128)} custom-call(bf16[2048,128]{1,0:T(8,128)(2,1)} %get-tuple-element.56.grads, f32[40,128]{1,0:T(8,128)} %get-tuple-element.57.factor_grads, f32[8,33]{1,0:T(8,128)} %bitcast.16, f32[8,64]{1,0:T(8,128)} %refs_1_.1), custom_call_target="tpu_custom_call" | custom-call | tf_op jit(solution)/shard_map/reduce_gradients/pallas_call | solution.py:597
  78.8 1.8 %update_weights.1 = (f32[1,1]{1,0:T(1,128)}, f32[1,1]{1,0:T(1,128)}, f32[1,1]{1,0:T(1,128)}, f32[8,33]{1,0:T(8,128)}, f32[8,64]{1,0:T(8,128)}, /*index=5*/f32[8,...) custom-call(s32[4,384]{1,0:T(4,128)} %seg_v.3, ...), custom_call_target="tpu_custom_call" | custom-call | tf_op jit(solution)/shard_map/update_weights/pallas_call | solution.py:633

commit v2 on v1

v2 whole, which is shorter than its diff:
```python
import functools

import jax
import jax.numpy as jnp
from jax import lax
from jax.experimental import pallas as pl
from jax.experimental.pallas import tpu as pltpu
from jax.sharding import PartitionSpec as P

norm_eps = 1e-05
clip_level = 0.001
beta_one = 0.9
beta_two = 0.999
adam_eps = 1e-10
decay_rate = 0.01
step_count = 10.0
rates = (0.5, 0.016, 0.016, 0.044, 0.044, 0.044, 0.5)

f32 = jnp.float32
bf16 = jnp.bfloat16
MESH = pl.DeviceIdType.MESH
VMEM = pltpu.VMEM
LIMIT = 56 * 1024 * 1024

vocab = 33
kinds = 40
groups = 34
table = groups * kinds
own_rows = 12
own = own_rows * kinds
parts_all = groups + own_rows
bins = 64
wide_size = 16
depth_size = 4
length = 384


def dot(a, b, axis_a, axis_b, precision=None):
    return lax.dot_general(
        a, b, (((axis_a,), (axis_b,)), ((), ())), precision=precision, preferred_element_type=f32
    )


def rounded(values):
    return values.astype(bf16).astype(f32)


def halves(values):
    high = values.astype(bf16)
    return high, (values - high.astype(f32)).astype(bf16)


def whole_sum(values):
    return jnp.sum(jnp.sum(values, axis=1, keepdims=True), axis=0, keepdims=True)


def step_kernel(
    tok_s, seg_s, tok_v, seg_v, tgt, emb, ab, outer, tri, mix, dist, gain,
    out,
    pack, tstage, stage, taken, ea, ea_taken, targets_in, source, gathered,
    weights, gram, tg, u, z, xhat, rstd, zn, sb, pb, tb,
    hist, many, wa, xi, ri, zr, sr, pr, x, dx, dz1, gr, gb,
    dpt, dpr, dzt, dzr, du, grads, packed, other, sent, taken_w, sum_z, taken_z,
    d_block, d_other, d_half, d_wide, d_sum, d_depth, d_final, d_partner, d_all, square, squares,
    sz, rz, sy, ry, sg, rg, st, rt, sc, rc, s1, r1, s2, r2, s3, r3, s4, r4, s5, r5, s6, r6, s7, r7, s8, r8,
):
    wide = lax.axis_index("wide")
    narrow = lax.axis_index("narrow")
    depth = narrow // 2
    core = lax.rem(narrow, 2)
    partner = (wide, depth * 2 + 1 - core)
    deep = [(wide, lax.rem(depth + k, depth_size) * 2 + core) for k in range(1, depth_size)]
    flat = [(lax.rem(wide + k, wide_size), narrow) for k in range(1, wide_size)]

    barrier = pltpu.get_barrier_semaphore()
    for peer in [partner] + deep + flat:
        pl.semaphore_signal(barrier, inc=1, device_id=peer, device_id_type=MESH)

    def remote(source_ref, target_ref, send, receive, peer):
        return pltpu.make_async_remote_copy(
            src_ref=source_ref, dst_ref=target_ref, send_sem=send, recv_sem=receive,
            device_id=peer, device_id_type=MESH,
        )

    def start(copies):
        for copy in copies:
            copy.start()
        return copies

    def wait(copies):
        for copy in copies:
            copy.wait()

    pack[...] = jnp.zeros_like(pack)
    pack[0:8, :] = outer[...]
    for m in range(5):
        pack[8 + m : 9 + m, :] = tri[:, 128 * m : 128 * m + 128]
    pack[13:14, :] = mix[...]
    pack[14:15, 0:64] = dist[...]
    pack[14:15, 64:66] = gain[...]
    low = pack[...].astype(bf16)
    tstage[...] = jnp.zeros_like(tstage)
    for m in range(depth_size):
        tstage[m, :, 0:48] = tgt[m, 0:16, :].astype(f32)
        tstage[m, :, 64:112] = tgt[m, 8:24, :].astype(f32)
        stage[m, 0:16, :] = low
        stage[m, 16:32, :] = tstage[m].astype(bf16)
    ea[...] = jnp.zeros_like(ea)
    ea[:, 0:vocab] = rounded(emb[...])
    ea[:, 64:128] = rounded(ab[...])
    pl.semaphore_wait(barrier, 1 + len(deep) + len(flat))

    copies = []
    for k, peer in enumerate(deep):
        copies.append(remote(stage.at[peer[1] // 2], taken.at[depth], sz.at[k], rz.at[k], peer))
        copies.append(remote(ea, ea_taken.at[depth], sy.at[k], ry.at[k], peer))
    start(copies)
    taken[depth] = stage[depth]
    ea_taken[depth] = ea[...]
    wait(copies)
    for m in range(depth_size):
        source[16 * m : 16 * m + 16, :] = taken[m, 0:16, :]
        targets_in[core, m] = taken[m, 16:32, :]
    source[64:96, :] = jnp.concatenate([ea_taken[m] for m in range(depth_size)], axis=0).astype(bf16)
    wide_copies = start(
        [
            remote(source, gathered.at[core, wide], sg.at[k], rg.at[k], peer)
            for k, peer in enumerate(flat)
        ]
    )
    moved = start([remote(targets_in.at[core], targets_in.at[core], st, rt, partner)])
    gathered[core, wide] = source[...]
    core_copies = start(
        [remote(source, gathered.at[core, wide], sc.at[0], rc.at[0], partner)]
    )

    wait(moved)
    for m in range(depth_size):
        for side in range(2):
            piece = targets_in[side, m].astype(f32)
            piece = jnp.where(core == 0, piece[:, 0:48], piece[:, 64:112])
            at = 48 * (2 * m + side)
            tg[:, at : at + 48] = piece
    row0 = wide * 24 + core * own_rows
    tok_row = tok_v[pl.ds(depth, 1), :]
    seg_row = seg_v[pl.ds(depth, 1), :]
    hot = (lax.broadcasted_iota(jnp.int32, (kinds, length), 0) == tok_row).astype(f32).astype(bf16)
    bin_of = lax.broadcasted_iota(jnp.int32, (bins, length), 0).astype(f32)
    line = lax.broadcasted_iota(jnp.int32, (48, kinds), 0)
    kind_of = line
    for i in range(own_rows):
        kind_of = jnp.where(line == groups + i, tok_s[depth, row0 + i], kind_of)
    pick = (kind_of == lax.broadcasted_iota(jnp.int32, (48, kinds), 1)).astype(f32).astype(bf16)
    for i in range(own_rows):
        here = slice(kinds * i, kinds * i + kinds)
        wanted = jnp.where(seg_row == seg_s[depth, row0 + i], tg[pl.ds(4 * core + i, 1), :], -1.0)
        counts = dot(hot, (bin_of == wanted).astype(f32).astype(bf16), 1, 1)
        hist[here, :] = counts
        many[here, :] = jnp.broadcast_to(jnp.sum(counts, -1, keepdims=True), (kinds, 128))
    count = jnp.zeros((4, 1), f32)
    for s in range(6):
        members = jnp.sum((seg_v[...] == s).astype(f32), axis=1, keepdims=True)
        count = count + members * members
    count = jnp.sum(count, axis=0, keepdims=True)

    for k, copy in enumerate(wide_copies):
        copy.wait_recv()
        slot = gathered.at[core, lax.rem(wide + wide_size - 1 - k, wide_size)]
        core_copies += start([remote(slot, slot, sc.at[k + 1], rc.at[k + 1], partner)])
    for copy in wide_copies:
        copy.wait_send()
    wait(core_copies)

    for side in range(2):
        for m in range(wide_size):
            for deep_at in range(depth_size):
                at = 16 * (8 * m + 2 * deep_at + side)
                weights[at : at + 16, :] = gathered[side, m, 16 * deep_at : 16 * deep_at + 16, :].astype(f32)
    shards = gathered[:, :, 64:96, :].reshape(2 * wide_size * 32, 128)
    gram[...] = dot(shards, shards, 0, 0)
    a = dot(pick, gram[0:kinds, 64:96].astype(bf16), 1, 0).astype(bf16)
    b = gram[0:kinds, 96:128].astype(bf16)
    w_outer = jnp.concatenate(
        [weights[pl.ds(16 * (q // 8) + q % 8, 32, stride=64), :] for q in range(32)], axis=1
    ).astype(bf16)
    w_own = jnp.concatenate(
        [weights[pl.ds(8 + m, 128, stride=16), :] for m in (0, 1, 4)], axis=1
    ).astype(bf16)
    w_other = jnp.concatenate(
        [weights[pl.ds(8 + m, 128, stride=16), :] for m in (2, 3)], axis=1
    ).astype(bf16)
    w_mix = weights[pl.ds(13, 128, stride=16), :].astype(bf16)
    tail_t = weights[pl.ds(14, 128, stride=16), :].T
    dist_t = tail_t[0:bins, :].astype(bf16)
    gain_in = tail_t[64:65, :]
    gain_mid = tail_t[65:66, :]

    u_q = rounded(dot(a, w_outer, 1, 0))
    for q in range(32):
        u[pl.ds(q, 48, stride=32), :] = u_q[:, 128 * q : 128 * q + 128]
    u_all = jnp.concatenate([u[32 * t : 32 * t + 32, :] for t in range(parts_all)], axis=1).astype(bf16)
    z_cat = dot(b, u_all, 1, 0)
    for t in range(parts_all):
        z[kinds * t : kinds * t + kinds, :] = z_cat[:, 128 * t : 128 * t + 128]

    chunk = 272
    tb[table:, :] = jnp.zeros((kinds * kinds - table, 128), f32)

    def forward(step, carry):
        at = pl.ds(pl.multiple_of(step * chunk, 16), chunk)
        values = z[at, :]
        center = values - jnp.mean(values, -1, keepdims=True)
        inverse = lax.rsqrt(jnp.mean(center * center, -1, keepdims=True) + norm_eps)
        scaled = center * inverse
        normed = (scaled * gain_in).astype(bf16)
        xhat[at, :] = scaled
        rstd[at, :] = jnp.broadcast_to(inverse, scaled.shape)
        zn[at, :] = normed
        projected = dot(normed, w_other, 1, 0)
        gate = jax.nn.sigmoid(projected[:, 0:128])
        value = projected[:, 128:256]
        sb[at, :] = gate
        pb[at, :] = value
        tb[at, :] = rounded(gate * value)
        return carry

    lax.fori_loop(0, table // chunk, forward, 0)

    values = z[table:, :]
    center = values - jnp.mean(values, -1, keepdims=True)
    inverse = lax.rsqrt(jnp.mean(center * center, -1, keepdims=True) + norm_eps)
    scaled = center * inverse
    xi[...] = scaled
    ri[...] = jnp.broadcast_to(inverse, scaled.shape)
    normed = (scaled * gain_in).astype(bf16)
    zr[...] = normed
    projected = dot(normed, w_own, 1, 0)
    gate = jax.nn.sigmoid(projected[:, 0:128])
    value = projected[:, 128:256]
    sr[...] = gate
    pr[...] = value
    wa[...] = many[...] * rounded(gate * value)
    gate_out = jax.nn.sigmoid(projected[:, 256:384])

    for group in range(own_rows // 4):
        mine = range(4 * group, 4 * group + 4)

        def product(v, sums, mine=mine):
            edge = tb[pl.ds(v, kinds, stride=kinds), :]
            return tuple(
                total + wa[pl.ds(kinds * i + v, 1), :] * edge for total, i in zip(sums, mine)
            )

        sums = lax.fori_loop(0, vocab, product, (jnp.zeros((kinds, 128), f32),) * 4)
        for total, i in zip(sums, mine):
            x[kinds * i : kinds * i + kinds, :] = total

    values = x[...]
    center = values - jnp.mean(values, -1, keepdims=True)
    inverse = lax.rsqrt(jnp.mean(center * center, -1, keepdims=True) + norm_eps)
    scaled = center * inverse
    mixed = (scaled * gain_mid).astype(bf16)
    branch = dot(mixed, w_mix, 1, 0)
    update = (z[table:, :] + gate_out * branch).astype(bf16)
    logits = dot(update, dist_t, 1, 1)
    top = jnp.max(logits, -1, keepdims=True)
    powers = jnp.exp(logits - top)
    power_sum = jnp.sum(powers, -1, keepdims=True)
    counts = hist[...]
    loss = jnp.sum(many[:, 0:1] * (jnp.log(power_sum) + top), axis=0, keepdims=True) - whole_sum(
        counts * logits
    )
    grad_logits = ((many[:, 0:bins] * (powers / power_sum) - counts) / count).astype(bf16)
    grad_dist_t = dot(grad_logits, update, 0, 0)
    grad_update = dot(grad_logits, dist_t, 1, 0)
    grad_branch = (grad_update * gate_out).astype(bf16)
    dz1[...] = grad_update
    dpr[:, 256:384] = (grad_update * branch * gate_out * (1.0 - gate_out)).astype(bf16)
    grad_mix = dot(mixed, grad_branch, 0, 0)
    grad_mixed = dot(grad_branch, w_mix, 1, 1)
    grad_gain_mid = jnp.sum(grad_mixed * scaled, axis=0, keepdims=True)
    grad_hat = grad_mixed * gain_mid
    dx[...] = inverse * (
        grad_hat
        - jnp.mean(grad_hat, -1, keepdims=True)
        - scaled * jnp.mean(grad_hat * scaled, -1, keepdims=True)
    )

    gb[...] = jnp.zeros_like(gb)
    for group in range(own_rows // 4):
        mine = range(4 * group, 4 * group + 4)
        weighted = [wa[kinds * i : kinds * i + kinds, :] for i in mine]

        def edges(t, sums, mine=mine, weighted=weighted):
            at = pl.ds(pl.multiple_of(t * kinds, 8), kinds)
            edge = tb[at, :]
            right = gb[at, :]
            news = []
            for total, i, left in zip(sums, mine, weighted):
                grad = dx[pl.ds(kinds * i + t, 1), :]
                news.append(total + grad * edge)
                right = right + grad * left
            gb[at, :] = right
            return tuple(news)

        sums = lax.fori_loop(0, vocab, edges, (jnp.zeros((kinds, 128), f32),) * 4)
        for total, i in zip(sums, mine):
            here = slice(kinds * i, kinds * i + kinds)
            gr[here, :] = total * many[here, :]

    def norm_back(grad_normed, scaled, inverse):
        grad_hat = grad_normed * gain_in
        return inverse * (
            grad_hat
            - jnp.mean(grad_hat, -1, keepdims=True)
            - scaled * jnp.mean(grad_hat * scaled, -1, keepdims=True)
        )

    gate = sr[...]
    grad = gr[...] * gate
    dpr[:, 0:128] = (grad * pr[...] * (1.0 - gate)).astype(bf16)
    dpr[:, 128:256] = grad.astype(bf16)
    grad_normed = dot(dpr[...], w_own, 1, 1)
    scaled = xi[...]
    grad_gain_in = jnp.sum(grad_normed * scaled, axis=0, keepdims=True)
    dzr[...] = dz1[...] + norm_back(grad_normed, scaled, ri[...])
    grad_tri_own = dot(zr[...], dpr[...], 0, 0)

    def backward(step, grad_gain):
        at = pl.ds(pl.multiple_of(step * chunk, 16), chunk)
        gate = sb[at, :]
        grad = gb[at, :] * gate
        dpt[at, 0:128] = (grad * pb[at, :] * (1.0 - gate)).astype(bf16)
        dpt[at, 128:256] = grad.astype(bf16)
        grad_normed = dot(dpt[at, :], w_other, 1, 1)
        scaled = xhat[at, :]
        dzt[at, :] = norm_back(grad_normed, scaled, rstd[at, :])
        return grad_gain + jnp.sum(grad_normed * scaled, axis=0, keepdims=True)

    grad_gain_in = lax.fori_loop(0, table // chunk, backward, grad_gain_in)
    grad_tri_other = dot(zn[...], dpt[...], 0, 0)

    blocks = [dzt[kinds * t : kinds * t + kinds, :] for t in range(groups)]
    blocks += [dzr[kinds * i : kinds * i + kinds, :] for i in range(own_rows)]
    dz_high, dz_low = halves(jnp.concatenate(blocks, axis=1))
    grad_u = dot(b, dz_high, 0, 0) + dot(b, dz_low, 0, 0)
    for t in range(parts_all):
        du[32 * t : 32 * t + 32, :] = grad_u[:, 128 * t : 128 * t + 128]
    du[32 * parts_all :, :] = jnp.zeros((32 * (48 - parts_all), 128), f32)
    grad_b = dot(dz_high, u_all, 1, 1) + dot(dz_low, u_all, 1, 1)
    du_high, du_low = halves(
        jnp.concatenate([du[pl.ds(q, 48, stride=32), :] for q in range(32)], axis=1)
    )
    grad_outer = dot(a, du_high, 0, 0) + dot(a, du_low, 0, 0)
    grad_a_high, grad_a_low = halves(dot(du_high, w_outer, 1, 1) + dot(du_low, w_outer, 1, 1))
    grad_a = dot(pick, grad_a_high, 0, 0) + dot(pick, grad_a_low, 0, 0)

    grads[...] = jnp.zeros_like(grads)
    for q in range(32):
        grads[pl.ds(16 * (q // 8) + q % 8, 32, stride=64), :] = grad_outer[:, 128 * q : 128 * q + 128]
    for at, m in enumerate((0, 1, 4)):
        grads[pl.ds(8 + m, 128, stride=16), :] = grad_tri_own[:, 128 * at : 128 * at + 128]
    for at, m in enumerate((2, 3)):
        grads[pl.ds(8 + m, 128, stride=16), :] = grad_tri_other[:, 128 * at : 128 * at + 128]
    grads[pl.ds(13, 128, stride=16), :] = grad_mix
    grads[pl.ds(14, 128, stride=16), :] = jnp.concatenate(
        [grad_dist_t, grad_gain_in, grad_gain_mid, jnp.zeros((62, 128), f32)], axis=0
    ).T
    for side in range(2):
        for m in range(wide_size):
            for deep_at in range(depth_size):
                at = 16 * (8 * m + 2 * deep_at + side)
                packed[side, m, 16 * deep_at : 16 * deep_at + 16, :] = grads[at : at + 16, :].astype(bf16)
    d_block[...] = jnp.zeros_like(d_block)
    for side, values in ((0, grad_a), (1, grad_b)):
        d_block[side, :, 0:32] = values[0:16]
        d_block[side, :, 32:64] = values[16:32]
        d_block[side, 0:8, 64:96] = values[32:40]
    d_block[0, 0:1, 96:97] = loss

    wait(
        start(
            [
                remote(packed.at[1 - core], other, s1, r1, partner),
                remote(d_block.at[1 - core], d_other, s2, r2, partner),
            ]
        )
    )
    for m in range(wide_size):
        sent[m] = (packed[core, m].astype(f32) + other[m].astype(f32)).astype(bf16)
    d_half[...] = d_block[core] + d_other[...]
    copies = []
    for k, peer in enumerate(flat):
        copies.append(remote(sent.at[peer[0]], taken_w.at[wide], s3.at[k], r3.at[k], peer))
        copies.append(remote(d_half, d_wide.at[wide], s4.at[k], r4.at[k], peer))
    start(copies)
    taken_w[wide] = sent[wide]
    d_wide[wide] = d_half[...]
    wait(copies)
    total = taken_w[0].astype(f32)
    small = d_wide[0]
    for m in range(1, wide_size):
        total = total + taken_w[m].astype(f32)
        small = small + d_wide[m]
    sum_z[...] = total.astype(bf16)
    d_sum[...] = small
    copies = []
    for k, peer in enumerate(deep):
        copies.append(remote(sum_z, taken_z.at[depth], s5.at[k], r5.at[k], peer))
        copies.append(remote(d_sum, d_depth.at[depth], s6.at[k], r6.at[k], peer))
    start(copies)
    taken_z[depth] = sum_z[...]
    d_depth[depth] = d_sum[...]
    wait(copies)
    total = taken_z[0].astype(f32)
    small = d_depth[0]
    for m in range(1, depth_size):
        total = total + taken_z[m].astype(f32)
        small = small + d_depth[m]
    lane = lax.broadcasted_iota(jnp.int32, (16, 128), 1)
    d_final[...] = jnp.where(lane == 100, whole_sum(total * total), small)
    copies = start([remote(d_final, d_partner, s7, r7, partner)])
    grads[0:64, :] = total
    out[0:16, :] = grads[pl.ds(pl.multiple_of(depth * 16, 16), 16), :]
    wait(copies)
    square[...] = jnp.broadcast_to(d_final[0:1, 100:101] + d_partner[0:1, 100:101], square.shape)
    copies = start(
        [remote(square, squares.at[wide], s8.at[k], r8.at[k], peer) for k, peer in enumerate(flat)]
    )
    squares[wide] = square[...]

    highest = lax.Precision.HIGHEST
    first = jnp.where(core == 0, d_final[...], d_partner[...])
    second = jnp.where(core == 0, d_partner[...], d_final[...])
    for side, values in ((0, first), (1, second)):
        at = slice(32 * side, 32 * side + 32)
        d_all[0:16, at] = values[:, 0:32]
        d_all[16:32, at] = values[:, 32:64]
        d_all[32:40, at] = values[0:8, 64:96]
    d_total = d_all[...]
    out[16:24, :] = jnp.zeros((8, 128), f32)
    out[24:32, :] = jnp.zeros((8, 128), f32)
    out[16:24, 0:kinds] = dot(ea[:, 64:128], d_total, 1, 1, highest)
    out[24:32, 0:64] = dot(ea[:, 0:kinds], d_total, 1, 0, highest)
    extra = whole_sum(dot(gram[0:kinds, 0:kinds], d_total, 1, 0, highest) * d_total)
    extra += whole_sum(dot(d_total, gram[64:128, 64:128], 1, 0, highest) * d_total)
    out[40:48, :] = jnp.broadcast_to(first[0:1, 96:97], (8, 128))
    wait(copies)
    total = squares[0]
    for m in range(1, wide_size):
        total = total + squares[m]
    out[32:40, :] = total + extra


def update_kernel(seg_v, reduced, *refs):
    weights, firsts, seconds = refs[0:7], refs[7:14], refs[14:21]
    loss_out, count_out, norm_out = refs[21:24]
    news, moms, vels = refs[24:31], refs[31:38], refs[38:45]
    count = jnp.zeros((4, 1), f32)
    for s in range(6):
        members = jnp.sum((seg_v[...] == s).astype(f32), axis=1, keepdims=True)
        count = count + members * members
    count_out[...] = jnp.sum(count, axis=0, keepdims=True)
    norm = jnp.sqrt(reduced[32:33, 0:1])
    norm_out[...] = norm
    loss_out[...] = reduced[40:41, 0:1]
    scale = jnp.minimum(1.0, clip_level / norm)
    tri = jnp.concatenate([reduced[8 + m : 9 + m, :] for m in range(5)], axis=1)
    grads = (
        reduced[16:24, 0:vocab],
        reduced[24:32, 0:64],
        reduced[0:8, :],
        tri,
        reduced[13:14, :],
        reduced[14:15, 0:64],
        reduced[14:15, 64:66],
    )
    for at, rate in enumerate(rates):
        clipped = grads[at] * scale
        weight = weights[at][...]
        first = beta_one * firsts[at][...] + (1.0 - beta_one) * clipped
        second = beta_two * seconds[at][...] + (1.0 - beta_two) * clipped * clipped
        ratio = (
            first
            / (1.0 - beta_one**step_count)
            / (jnp.sqrt(second / (1.0 - beta_two**step_count)) + adam_eps)
        )
        news[at][...] = weight - rate * (ratio + decay_rate * weight)
        moms[at][...] = first
        vels[at][...] = second


def shape(*dims, dtype=f32):
    return jax.ShapeDtypeStruct(dims, dtype)


in_vmem = pl.BlockSpec(memory_space=pltpu.VMEM)
in_smem = pl.BlockSpec(memory_space=pltpu.SMEM)


def shape(*dims, dtype=f32):
    return jax.ShapeDtypeStruct(dims, dtype)


in_vmem = pl.BlockSpec(memory_space=pltpu.VMEM)
in_smem = pl.BlockSpec(memory_space=pltpu.SMEM)


def step_call(*args):
    def sems(*dims):
        return [pltpu.SemaphoreType.DMA(dims), pltpu.SemaphoreType.DMA(dims)]

    def one():
        return [pltpu.SemaphoreType.DMA, pltpu.SemaphoreType.DMA]

    full = VMEM((table, 128), f32)
    mine = VMEM((own, 128), f32)
    block = VMEM((16, 128), f32)
    return pl.pallas_call(
        step_kernel,
        out_shape=shape(48, 128),
        in_specs=[in_smem] * 2 + [in_vmem] * (len(args) - 2),
        out_specs=in_vmem,
        scratch_shapes=[
            block,
            VMEM((depth_size, 16, 128), f32),
            VMEM((depth_size, 32, 128), bf16),
            VMEM((depth_size, 32, 128), bf16),
            VMEM((8, 128), f32),
            VMEM((depth_size, 8, 128), f32),
            VMEM((2, depth_size, 16, 128), bf16),
            VMEM((96, 128), bf16),
            VMEM((2, wide_size, 96, 128), bf16),
            VMEM((2048, 128), f32),
            VMEM((128, 128), f32),
            VMEM((16, length), f32),
            VMEM((32 * 48, 128), f32),
            VMEM((kinds * parts_all, 128), f32),
            full, full,
            VMEM((table, 128), bf16),
            full, full,
            VMEM((kinds * kinds, 128), f32),
            VMEM((own, bins), f32),
            mine, mine, mine, mine,
            VMEM((own, 128), bf16),
            mine, mine, mine, mine, mine, mine,
            full,
            VMEM((table, 256), bf16),
            VMEM((own, 384), bf16),
            full,
            mine,
            VMEM((32 * 48, 128), f32),
            VMEM((2048, 128), f32),
            VMEM((2, wide_size, 64, 128), bf16),
            VMEM((wide_size, 64, 128), bf16),
            VMEM((wide_size, 64, 128), bf16),
            VMEM((wide_size, 64, 128), bf16),
            VMEM((64, 128), bf16),
            VMEM((depth_size, 64, 128), bf16),
            VMEM((2, 16, 128), f32),
            block, block,
            VMEM((wide_size, 16, 128), f32),
            block,
            VMEM((depth_size, 16, 128), f32),
            block, block,
            VMEM((kinds, 64), f32),
            VMEM((8, 128), f32),
            VMEM((wide_size, 8, 128), f32),
            *sems(depth_size), *sems(depth_size), *sems(wide_size), *one(), *sems(wide_size),
            *one(), *one(), *sems(wide_size), *sems(wide_size), *sems(depth_size), *sems(depth_size),
            *one(), *sems(wide_size),
        ],
        compiler_params=pltpu.CompilerParams(
            collective_id=0, has_side_effects=True, vmem_limit_bytes=LIMIT
        ),
        name="pair_step",
    )(*args)


def local(tokens, segments, targets, *state):
    state = list(state)
    for at in (0, 6, 7, 13, 14, 20):
        state[at] = state[at].T
    masters = state[0:7]
    reduced = step_call(tokens, segments, tokens, segments, targets, *masters)
    shapes = [shape(*w.shape) for w in masters]
    outs = pl.pallas_call(
        update_kernel,
        out_shape=[shape(1, 1)] * 3 + shapes * 3,
        in_specs=[in_vmem] * (2 + 21),
        out_specs=[in_vmem] * 24,
        name="update_weights",
    )(segments, reduced, *state)
    outs = [value.reshape(()) for value in outs[0:3]] + list(outs[3:])
    for at in (3, 9, 10, 16, 17, 23):
        outs[at] = outs[at].T
    return tuple(outs)


def solution(mesh):
    both = ("wide", "narrow")
    whole = (P(None, both), P(both, None), P(both, None), P(both, None), P(both, None), P(both, None), P(None, both))
    return jax.shard_map(
        local,
        mesh=mesh,
        in_specs=(P(), P(), P(None, "wide", "narrow")) + whole * 3,
        out_specs=(P(), P(), P()) + whole * 3,
        check_vma=False,
    )
```

time: 80.9 us -> 57.2 us (0.71)
  Pallas kernels: 80 us -> 56.3 us
    pallas_call x3 -> x1, Pallas kernels: 78.1 us -> 54.5 us  [step_call(): pl.pallas_call(step_kernel, out_shape=shape(48, 128), in_specs=[in_smem]...]
where the time goes in v2:
time: 57.2 us; the launch traced here: 56.9 us
  Pallas kernels  56.3 us (98%)
  between operations  0.67 us (1%)
    pallas_call x1, Pallas kernels, step_call(): pl.pallas_call(step_kernel, out_shape=shape(48, 128), in_specs=[in_smem]...  54.5 us
    pallas_call x1, Pallas kernels, local(): pl.pallas_call(update_kernel, out_shape=[shape(1, 1)] * 3 + shapes * 3, i...  1.81 us

profile of v2, /device:TPU:1, one launch (start us, length us, event | category | flops | bytes accessed | tf_op | source)
XLA Modules:
  0.0 56.9 jit_solution(10195303789016503498)
XLA Ops:
  0.7 54.5 %pair_step.1.reduced = f32[48,128]{1,0:T(8,128)} custom-call(s32[4,384]{1,0:T(4,128)} %tok_v.1, s32[4,384]{1,0:T(4,128)} %seg_v.3, s32[4,384]{1,0:T(4,128)} %tok_v.1, s32[4,384]{1,0:T(4,128)} %seg_v.3, s32[4,24,48]{2,1,0:T(8,128)} %tgt.1, f32[8,33]{1,0:T(8,128)} %bitcast.15, f32[8,64]{1,0:T(8,128)} %refs_1_.1, f32[8,128]{1,0:T(8,128)} %refs_2_.1, ...), custom_call_target="tpu_custom_call" | custom-call | tf_op jit(solution)/shard_map/pair_step/pallas_call | solution.py:519
  55.1 1.8 %update_weights.1 = (f32[1,1]{1,0:T(1,128)}, f32[1,1]{1,0:T(1,128)}, f32[1,1]{1,0:T(1,128)}, f32[8,33]{1,0:T(8,128)}, f32[8,64]{1,0:T(8,128)}, /*index=5*/f32[8,...) custom-call(s32[4,384]{1,0:T(4,128)} %seg_v.3, ...), custom_call_target="tpu_custom_call" | custom-call | tf_op jit(solution)/shard_map/update_weights/pallas_call | solution.py:587

commit v3 on v2

--- a/solution.py
+++ b/solution.py
@@ -54,27 +54,52 @@
     return jnp.sum(jnp.sum(values, axis=1, keepdims=True), axis=0, keepdims=True)
 
 
-def step_kernel(
-    tok_s, seg_s, tok_v, seg_v, tgt, emb, ab, outer, tri, mix, dist, gain,
-    out,
-    pack, tstage, stage, taken, ea, ea_taken, targets_in, source, gathered,
-    weights, gram, tg, u, z, xhat, rstd, zn, sb, pb, tb,
-    hist, many, wa, xi, ri, zr, sr, pr, x, dx, dz1, gr, gb,
-    dpt, dpr, dzt, dzr, du, grads, packed, other, sent, taken_w, sum_z, taken_z,
-    d_block, d_other, d_half, d_wide, d_sum, d_depth, d_final, d_partner, d_all, square, squares,
-    sz, rz, sy, ry, sg, rg, st, rt, sc, rc, s1, r1, s2, r2, s3, r3, s4, r4, s5, r5, s6, r6, s7, r7, s8, r8,
-):
+def hops(step):
+    return sum(min(part, 4 - part) for part in step)
+
+
+flat_steps = sorted(
+    [(dy, dx) for dy in range(4) for dx in range(4) if (dy, dx) != (0, 0)], key=hops, reverse=True
+)
+deep_steps = (2, 1, 3)
+
+
+def step_kernel(*refs):
+    inputs, refs = refs[:24], refs[24:]
+    out, refs = refs[0], refs[1:]
+    held, refs = refs[:24], refs[24:]
+    (
+        tok_s, seg_s, loaded,
+        state, tstage, stage, taken, ea, targets_in, source, gathered,
+        weights, gram, tg, u, z, xhat, rstd, zn, sb, pb, tb,
+        hist, many, wa, xi, ri, zr, sr, pr, x, dx, dz1, gr, gb,
+        dpt, dpr, dzt, dzr, du, grads, packed, other, sent, taken_w, sum_z, taken_z,
+        d_block, d_other, d_final, d_partner, d_all, square, squares, square_c, square_p,
+        sz, rz, sg, rg, st, rt, sc, rc, s1, r1, s2, r2, s3, r3, s5, r5, s7, r7, s8, r8, s9, r9,
+    ) = refs
     wide = lax.axis_index("wide")
     narrow = lax.axis_index("narrow")
     depth = narrow // 2
     core = lax.rem(narrow, 2)
+    row, column = wide // 4, lax.rem(wide, 4)
+
+    def at_step(dy, dx):
+        return lax.rem(row + dy, 4) * 4 + lax.rem(column + dx, 4)
+
     partner = (wide, depth * 2 + 1 - core)
-    deep = [(wide, lax.rem(depth + k, depth_size) * 2 + core) for k in range(1, depth_size)]
-    flat = [(lax.rem(wide + k, wide_size), narrow) for k in range(1, wide_size)]
+    deep = [(wide, lax.rem(depth + k, depth_size) * 2 + core) for k in deep_steps]
+    flat = [(at_step(dy, dx), narrow) for dy, dx in flat_steps]
+    flat_from = [at_step(4 - dy, 4 - dx) for dy, dx in flat_steps]
 
     barrier = pltpu.get_barrier_semaphore()
-    for peer in [partner] + deep + flat:
+    for peer in flat + deep + [partner]:
         pl.semaphore_signal(barrier, inc=1, device_id=peer, device_id_type=MESH)
+
+    loads = [pltpu.make_async_copy(a, b, loaded.at[k]) for k, (a, b) in enumerate(zip(inputs, held))]
+    loads.append(pltpu.make_async_copy(inputs[0], tok_s, loaded.at[24]))
+    loads.append(pltpu.make_async_copy(inputs[1], seg_s, loaded.at[25]))
+    for load in loads:
+        load.start()
 
     def remote(source_ref, target_ref, send, receive, peer):
         return pltpu.make_async_remote_copy(
@@ -91,37 +116,49 @@
         for copy in copies:
             copy.wait()
 
-    pack[...] = jnp.zeros_like(pack)
-    pack[0:8, :] = outer[...]
-    for m in range(5):
-        pack[8 + m : 9 + m, :] = tri[:, 128 * m : 128 * m + 128]
-    pack[13:14, :] = mix[...]
-    pack[14:15, 0:64] = dist[...]
-    pack[14:15, 64:66] = gain[...]
-    low = pack[...].astype(bf16)
+    state[...] = jnp.zeros_like(state)
     tstage[...] = jnp.zeros_like(tstage)
+    stage[...] = jnp.zeros_like(stage)
+    ea[...] = jnp.zeros_like(ea)
+    for load in loads:
+        load.wait()
+    tok_v, seg_v, tgt = held[0:3]
+    for kind in range(3):
+        emb, ab, outer, tri, mix, dist, gain = held[3 + 7 * kind : 10 + 7 * kind]
+        state[kind, 0:8, :] = outer[...]
+        for m in range(5):
+            state[kind, 8 + m : 9 + m, :] = tri[:, 128 * m : 128 * m + 128]
+        state[kind, 13:14, :] = mix[...]
+        state[kind, 14:15, 0:64] = dist[...]
+        state[kind, 14:15, 64:66] = gain[...]
+        state[kind, 16:24, 0:vocab] = emb[...]
+        state[kind, 24:32, 0:64] = ab[...]
+    ea[0:8, 0:vocab] = rounded(held[3][...])
+    ea[0:8, 64:128] = rounded(held[4][...])
+    low = state[0, 0:16, :].astype(bf16)
+    low_ea = ea[...].astype(bf16)
     for m in range(depth_size):
         tstage[m, :, 0:48] = tgt[m, 0:16, :].astype(f32)
         tstage[m, :, 64:112] = tgt[m, 8:24, :].astype(f32)
         stage[m, 0:16, :] = low
         stage[m, 16:32, :] = tstage[m].astype(bf16)
-    ea[...] = jnp.zeros_like(ea)
-    ea[:, 0:vocab] = rounded(emb[...])
-    ea[:, 64:128] = rounded(ab[...])
+        stage[m, 32:48, :] = low_ea
     pl.semaphore_wait(barrier, 1 + len(deep) + len(flat))
 
-    copies = []
-    for k, peer in enumerate(deep):
-        copies.append(remote(stage.at[peer[1] // 2], taken.at[depth], sz.at[k], rz.at[k], peer))
-        copies.append(remote(ea, ea_taken.at[depth], sy.at[k], ry.at[k], peer))
-    start(copies)
+    copies = start(
+        [
+            remote(stage.at[peer[1] // 2], taken.at[depth], sz.at[k], rz.at[k], peer)
+            for k, peer in enumerate(deep)
+        ]
+    )
     taken[depth] = stage[depth]
-    ea_taken[depth] = ea[...]
     wait(copies)
     for m in range(depth_size):
         source[16 * m : 16 * m + 16, :] = taken[m, 0:16, :]
         targets_in[core, m] = taken[m, 16:32, :]
-    source[64:96, :] = jnp.concatenate([ea_taken[m] for m in range(depth_size)], axis=0).astype(bf16)
+    source[64:96, :] = jnp.concatenate(
+        [taken[m, 32:48, :].astype(f32)[0:8] for m in range(depth_size)], axis=0
+    ).astype(bf16)
     wide_copies = start(
         [
             remote(source, gathered.at[core, wide], sg.at[k], rg.at[k], peer)
@@ -163,9 +200,9 @@
         count = count + members * members
     count = jnp.sum(count, axis=0, keepdims=True)
 
-    for k, copy in enumerate(wide_copies):
-        copy.wait_recv()
-        slot = gathered.at[core, lax.rem(wide + wide_size - 1 - k, wide_size)]
+    for k in reversed(range(wide_size - 1)):
+        wide_copies[k].wait_recv()
+        slot = gathered.at[core, flat_from[k]]
         core_copies += start([remote(slot, slot, sc.at[k + 1], rc.at[k + 1], partner)])
     for copy in wide_copies:
         copy.wait_send()
@@ -224,7 +261,7 @@
         tb[at, :] = rounded(gate * value)
         return carry
 
-    lax.fori_loop(0, table // chunk, forward, 0)
+    lax.fori_loop(0, table // chunk, forward, 0, unroll=True)
 
     values = z[table:, :]
     center = values - jnp.mean(values, -1, keepdims=True)
@@ -251,7 +288,7 @@
                 total + wa[pl.ds(kinds * i + v, 1), :] * edge for total, i in zip(sums, mine)
             )
 
-        sums = lax.fori_loop(0, vocab, product, (jnp.zeros((kinds, 128), f32),) * 4)
+        sums = lax.fori_loop(0, vocab, product, (jnp.zeros((kinds, 128), f32),) * 4, unroll=11)
         for total, i in zip(sums, mine):
             x[kinds * i : kinds * i + kinds, :] = total
 
@@ -303,7 +340,7 @@
             gb[at, :] = right
             return tuple(news)
 
-        sums = lax.fori_loop(0, vocab, edges, (jnp.zeros((kinds, 128), f32),) * 4)
+        sums = lax.fori_loop(0, vocab, edges, (jnp.zeros((kinds, 128), f32),) * 4, unroll=11)
         for total, i in zip(sums, mine):
             here = slice(kinds * i, kinds * i + kinds)
             gr[here, :] = total * many[here, :]
@@ -337,7 +374,7 @@
         dzt[at, :] = norm_back(grad_normed, scaled, rstd[at, :])
         return grad_gain + jnp.sum(grad_normed * scaled, axis=0, keepdims=True)
 
-    grad_gain_in = lax.fori_loop(0, table // chunk, backward, grad_gain_in)
+    grad_gain_in = lax.fori_loop(0, table // chunk, backward, grad_gain_in, unroll=True)
     grad_tri_other = dot(zn[...], dpt[...], 0, 0)
 
     blocks = [dzt[kinds * t : kinds * t + kinds, :] for t in range(groups)]
@@ -386,49 +423,53 @@
             ]
         )
     )
-    for m in range(wide_size):
-        sent[m] = (packed[core, m].astype(f32) + other[m].astype(f32)).astype(bf16)
-    d_half[...] = d_block[core] + d_other[...]
+    lane = lax.broadcasted_iota(jnp.int32, (16, 128), 1)
+
+    def split_loss(block):
+        held_loss = jnp.sum(jnp.where((lane >= 96) & (lane < 99), block, 0.0), axis=1, keepdims=True)
+        high = rounded(held_loss)
+        middle = rounded(held_loss - high)
+        block = jnp.where(lane == 96, high, block)
+        block = jnp.where(lane == 97, middle, block)
+        return jnp.where(lane == 98, held_loss - high - middle, block).astype(bf16)
+
+    small = split_loss(d_block[core] + d_other[...])
     copies = []
     for k, peer in enumerate(flat):
-        copies.append(remote(sent.at[peer[0]], taken_w.at[wide], s3.at[k], r3.at[k], peer))
-        copies.append(remote(d_half, d_wide.at[wide], s4.at[k], r4.at[k], peer))
-    start(copies)
-    taken_w[wide] = sent[wide]
-    d_wide[wide] = d_half[...]
+        sent[peer[0], 0:64, :] = (
+            packed[core, peer[0]].astype(f32) + other[peer[0]].astype(f32)
+        ).astype(bf16)
+        sent[peer[0], 64:80, :] = small
+        copies += start([remote(sent.at[peer[0]], taken_w.at[wide], s3.at[k], r3.at[k], peer)])
+    taken_w[wide, 0:64, :] = (packed[core, wide].astype(f32) + other[wide].astype(f32)).astype(bf16)
+    taken_w[wide, 64:80, :] = small
     wait(copies)
     total = taken_w[0].astype(f32)
-    small = d_wide[0]
     for m in range(1, wide_size):
         total = total + taken_w[m].astype(f32)
-        small = small + d_wide[m]
-    sum_z[...] = total.astype(bf16)
-    d_sum[...] = small
-    copies = []
-    for k, peer in enumerate(deep):
-        copies.append(remote(sum_z, taken_z.at[depth], s5.at[k], r5.at[k], peer))
-        copies.append(remote(d_sum, d_depth.at[depth], s6.at[k], r6.at[k], peer))
-    start(copies)
+    sum_z[0:64, :] = total[0:64].astype(bf16)
+    sum_z[64:80, :] = split_loss(total[64:80])
+    copies = start(
+        [
+            remote(sum_z, taken_z.at[depth], s5.at[k], r5.at[k], peer)
+            for k, peer in enumerate(deep)
+        ]
+    )
     taken_z[depth] = sum_z[...]
-    d_depth[depth] = d_sum[...]
     wait(copies)
     total = taken_z[0].astype(f32)
-    small = d_depth[0]
     for m in range(1, depth_size):
         total = total + taken_z[m].astype(f32)
-        small = small + d_depth[m]
-    lane = lax.broadcasted_iota(jnp.int32, (16, 128), 1)
-    d_final[...] = jnp.where(lane == 100, whole_sum(total * total), small)
-    copies = start([remote(d_final, d_partner, s7, r7, partner)])
-    grads[0:64, :] = total
-    out[0:16, :] = grads[pl.ds(pl.multiple_of(depth * 16, 16), 16), :]
-    wait(copies)
-    square[...] = jnp.broadcast_to(d_final[0:1, 100:101] + d_partner[0:1, 100:101], square.shape)
+    square[...] = jnp.broadcast_to(whole_sum(total[0:64] * total[0:64]), square.shape)
     copies = start(
         [remote(square, squares.at[wide], s8.at[k], r8.at[k], peer) for k, peer in enumerate(flat)]
     )
+    d_final[...] = total[64:80]
+    d_copies = start([remote(d_final, d_partner, s7, r7, partner)])
     squares[wide] = square[...]
-
+    grads[0:64, :] = total[0:64]
+
+    wait(d_copies)
     highest = lax.Precision.HIGHEST
     first = jnp.where(core == 0, d_final[...], d_partner[...])
     second = jnp.where(core == 0, d_partner[...], d_final[...])
@@ -438,56 +479,58 @@
         d_all[16:32, at] = values[:, 32:64]
         d_all[32:40, at] = values[0:8, 64:96]
     d_total = d_all[...]
-    out[16:24, :] = jnp.zeros((8, 128), f32)
-    out[24:32, :] = jnp.zeros((8, 128), f32)
-    out[16:24, 0:kinds] = dot(ea[:, 64:128], d_total, 1, 1, highest)
-    out[24:32, 0:64] = dot(ea[:, 0:kinds], d_total, 1, 0, highest)
+    grad = x
+    grad[0:16, :] = grads[pl.ds(pl.multiple_of(depth * 16, 16), 16), :]
+    grad[16:32, :] = jnp.zeros((16, 128), f32)
+    grad[16:24, 0:kinds] = dot(ea[0:8, 64:128], d_total, 1, 1, highest)
+    grad[24:32, 0:64] = dot(ea[0:8, 0:kinds], d_total, 1, 0, highest)
     extra = whole_sum(dot(gram[0:kinds, 0:kinds], d_total, 1, 0, highest) * d_total)
     extra += whole_sum(dot(d_total, gram[64:128, 64:128], 1, 0, highest) * d_total)
-    out[40:48, :] = jnp.broadcast_to(first[0:1, 96:97], (8, 128))
+    loss_sum = jnp.sum(first[0:1, 96:99], axis=1, keepdims=True)
+    line = lax.broadcasted_iota(jnp.int32, (32, 128), 0)
+    lane = lax.broadcasted_iota(jnp.int32, (32, 128), 1)
+    slow = (line < 8) | (line >= 24)
+    fast = ((line >= 16) & (line < 24)) | ((line == 14) & (lane >= 64))
+    rate = jnp.where(slow, rates[1], jnp.where(fast, rates[0], rates[3]))
+    weight = state[0]
+    first_part = beta_one * state[1]
+    second_part = beta_two * state[2]
     wait(copies)
     total = squares[0]
     for m in range(1, wide_size):
         total = total + squares[m]
-    out[32:40, :] = total + extra
-
-
-def update_kernel(seg_v, reduced, *refs):
-    weights, firsts, seconds = refs[0:7], refs[7:14], refs[14:21]
-    loss_out, count_out, norm_out = refs[21:24]
-    news, moms, vels = refs[24:31], refs[31:38], refs[38:45]
-    count = jnp.zeros((4, 1), f32)
-    for s in range(6):
-        members = jnp.sum((seg_v[...] == s).astype(f32), axis=1, keepdims=True)
-        count = count + members * members
-    count_out[...] = jnp.sum(count, axis=0, keepdims=True)
-    norm = jnp.sqrt(reduced[32:33, 0:1])
-    norm_out[...] = norm
-    loss_out[...] = reduced[40:41, 0:1]
-    scale = jnp.minimum(1.0, clip_level / norm)
-    tri = jnp.concatenate([reduced[8 + m : 9 + m, :] for m in range(5)], axis=1)
-    grads = (
-        reduced[16:24, 0:vocab],
-        reduced[24:32, 0:64],
-        reduced[0:8, :],
-        tri,
-        reduced[13:14, :],
-        reduced[14:15, 0:64],
-        reduced[14:15, 64:66],
-    )
-    for at, rate in enumerate(rates):
-        clipped = grads[at] * scale
-        weight = weights[at][...]
-        first = beta_one * firsts[at][...] + (1.0 - beta_one) * clipped
-        second = beta_two * seconds[at][...] + (1.0 - beta_two) * clipped * clipped
-        ratio = (
-            first
-            / (1.0 - beta_one**step_count)
-            / (jnp.sqrt(second / (1.0 - beta_two**step_count)) + adam_eps)
-        )
-        news[at][...] = weight - rate * (ratio + decay_rate * weight)
-        moms[at][...] = first
-        vels[at][...] = second
+    square_c[...] = total
+    wait(start([remote(square_c, square_p, s9, r9, partner)]))
+    norm = jnp.sqrt(square_c[0:1, 0:1] + square_p[0:1, 0:1] + extra)
+    clipped = grad[0:32, :] * jnp.minimum(1.0, clip_level / norm)
+    moment = first_part + (1.0 - beta_one) * clipped
+    speed = second_part + (1.0 - beta_two) * clipped * clipped
+    ratio = (
+        moment
+        / (1.0 - beta_one**step_count)
+        / (jnp.sqrt(speed / (1.0 - beta_two**step_count)) + adam_eps)
+    )
+    out[0:32, :] = weight - rate * (ratio + decay_rate * weight)
+    out[32:64, :] = moment
+    out[64:96, :] = speed
+    line = lax.broadcasted_iota(jnp.int32, (8, 128), 0)
+    out[96:104, :] = jnp.where(line == 0, loss_sum, jnp.where(line == 1, count, norm))
+
+
+def place_kernel(stepped, *outs):
+    for at in range(3):
+        outs[at][...] = stepped[96 + at : 97 + at, 0:1]
+    for kind in range(3):
+        emb, ab, outer, tri, mix, dist, gain = outs[3 + 7 * kind : 10 + 7 * kind]
+        base = 32 * kind
+        outer[...] = stepped[base : base + 8, :]
+        for m in range(5):
+            tri[:, 128 * m : 128 * m + 128] = stepped[base + 8 + m : base + 9 + m, :]
+        mix[...] = stepped[base + 13 : base + 14, :]
+        dist[...] = stepped[base + 14 : base + 15, 0:64]
+        gain[...] = stepped[base + 14 : base + 15, 64:66]
+        emb[...] = stepped[base + 16 : base + 24, 0:vocab]
+        ab[...] = stepped[base + 24 : base + 32, 0:64]
 
 
 def shape(*dims, dtype=f32):
@@ -495,15 +538,6 @@
 
 
 in_vmem = pl.BlockSpec(memory_space=pltpu.VMEM)
-in_smem = pl.BlockSpec(memory_space=pltpu.SMEM)
-
-
-def shape(*dims, dtype=f32):
-    return jax.ShapeDtypeStruct(dims, dtype)
-
-
-in_vmem = pl.BlockSpec(memory_space=pltpu.VMEM)
-in_smem = pl.BlockSpec(memory_space=pltpu.SMEM)
 
 
 def step_call(*args):
@@ -518,16 +552,18 @@
     block = VMEM((16, 128), f32)
     return pl.pallas_call(
         step_kernel,
-        out_shape=shape(48, 128),
-        in_specs=[in_smem] * 2 + [in_vmem] * (len(args) - 2),
+        out_shape=shape(104, 128),
+        in_specs=[pl.BlockSpec(memory_space=pl.ANY)] * len(args),
         out_specs=in_vmem,
         scratch_shapes=[
+            *[VMEM(arg.shape, arg.dtype) for arg in args],
+            pltpu.SMEM(args[0].shape, jnp.int32), pltpu.SMEM(args[1].shape, jnp.int32),
+            pltpu.SemaphoreType.DMA((26,)),
+            VMEM((3, 32, 128), f32),
+            VMEM((depth_size, 16, 128), f32),
+            VMEM((depth_size, 48, 128), bf16),
+            VMEM((depth_size, 48, 128), bf16),
             block,
-            VMEM((depth_size, 16, 128), f32),
-            VMEM((depth_size, 32, 128), bf16),
-            VMEM((depth_size, 32, 128), bf16),
-            VMEM((8, 128), f32),
-            VMEM((depth_size, 8, 128), f32),
             VMEM((2, depth_size, 16, 128), bf16),
             VMEM((96, 128), bf16),
             VMEM((2, wide_size, 96, 128), bf16),
@@ -553,22 +589,18 @@
             VMEM((2048, 128), f32),
             VMEM((2, wide_size, 64, 128), bf16),
             VMEM((wide_size, 64, 128), bf16),
-            VMEM((wide_size, 64, 128), bf16),
-            VMEM((wide_size, 64, 128), bf16),
-            VMEM((64, 128), bf16),
-            VMEM((depth_size, 64, 128), bf16),
+            VMEM((wide_size, 80, 128), bf16),
+            VMEM((wide_size, 80, 128), bf16),
+            VMEM((80, 128), bf16),
+            VMEM((depth_size, 80, 128), bf16),
             VMEM((2, 16, 128), f32),
-            block, block,
-            VMEM((wide_size, 16, 128), f32),
-            block,
-            VMEM((depth_size, 16, 128), f32),
-            block, block,
+            block, block, block,
             VMEM((kinds, 64), f32),
             VMEM((8, 128), f32),
             VMEM((wide_size, 8, 128), f32),
-            *sems(depth_size), *sems(depth_size), *sems(wide_size), *one(), *sems(wide_size),
-            *one(), *one(), *sems(wide_size), *sems(wide_size), *sems(depth_size), *sems(depth_size),
-            *one(), *sems(wide_size),
+            VMEM((8, 128), f32), VMEM((8, 128), f32),
+            *sems(depth_size), *sems(wide_size), *one(), *sems(wide_size),
+            *one(), *one(), *sems(wide_size), *sems(depth_size), *one(), *sems(wide_size), *one(),
         ],
         compiler_params=pltpu.CompilerParams(
             collective_id=0, has_side_effects=True, vmem_limit_bytes=LIMIT
@@ -581,16 +613,15 @@
     state = list(state)
     for at in (0, 6, 7, 13, 14, 20):
         state[at] = state[at].T
-    masters = state[0:7]
-    reduced = step_call(tokens, segments, tokens, segments, targets, *masters)
-    shapes = [shape(*w.shape) for w in masters]
+    stepped = step_call(tokens, segments, targets, *state)
+    shapes = [shape(*w.shape) for w in state[0:7]]
     outs = pl.pallas_call(
-        update_kernel,
+        place_kernel,
         out_shape=[shape(1, 1)] * 3 + shapes * 3,
-        in_specs=[in_vmem] * (2 + 21),
+        in_specs=[in_vmem],
         out_specs=[in_vmem] * 24,
-        name="update_weights",
-    )(segments, reduced, *state)
+        name="place_outputs",
+    )(stepped)
     outs = [value.reshape(()) for value in outs[0:3]] + list(outs[3:])
     for at in (3, 9, 10, 16, 17, 23):
         outs[at] = outs[at].T

time: 57.2 us -> 50.3 us (0.88)
  Pallas kernels: 56.3 us -> 49.4 us
    pallas_call x2, Pallas kernels: 56.3 us -> 49.4 us  [the longest x1 47.9 us: step_call(): pl.pallas_call(step_kernel, out_shape=shape(104, 128), in_specs=[pl.Block...]
where the time goes in v3:
time: 50.3 us; the launch traced here: 50 us
  Pallas kernels  49.4 us (98%)
  between operations  0.68 us (1%)
    pallas_call x1, Pallas kernels, step_call(): pl.pallas_call(step_kernel, out_shape=shape(104, 128), in_specs=[pl.Block...  47.9 us
    pallas_call x1, Pallas kernels, local(): pl.pallas_call(place_kernel, out_shape=[shape(1, 1)] * 3 + shapes * 3, in...  1.52 us

profile of v3, /device:TPU:1, one launch (start us, length us, event | category | flops | bytes accessed | tf_op | source)
XLA Modules:
  0.0 50.0 jit_solution(7870005261991121266)
XLA Ops:
  0.7 47.9 %pair_step.1.stepped = f32[104,128]{1,0:T(8,128)} custom-call(s32[4,384]{1,0:T(4,128)} %refs_0_.1, s32[4,384]{1,0:T(4,128)} %refs_1_.1, s32[4,24,48]{2,1,0:T(8,128)} %refs_2_.1, f32[8,33]{1,0:T(8,128)} %bitcast.15, f32[8,64]{1,0:T(8,128)} %refs_4_.1, f32[8,128]{1,0:T(8,128)} %refs_5_.1, f32[1,640]{1,0:T(1,128)} %refs_6_.1, f32[1,128]{1,0:T(1,128)} %refs_7_.1, ...), custom_call_target="tpu_custom_call" | custom-call | tf_op jit(solution)/shard_map/pair_step/pallas_call | solution.py:553
  48.5 1.5 %place_outputs.1 = (f32[1,1]{1,0:T(1,128)}, f32[1,1]{1,0:T(1,128)}, f32[1,1]{1,0:T(1,128)}, f32[8,33]{1,0:T(8,128)}, f32[8,64]{1,0:T(8,128)}, /*index=5*/f32[8,1...) custom-call(f32[104,128]{1,0:T(8,128)} %pair_step.1.stepped), custom_call_target="tpu_custom_call" | custom-call | tf_op jit(solution)/shard_map/place_outputs/pallas_call | solution.py:618

commit v4 on v3

--- a/solution.py
+++ b/solution.py
@@ -54,13 +54,7 @@
     return jnp.sum(jnp.sum(values, axis=1, keepdims=True), axis=0, keepdims=True)
 
 
-def hops(step):
-    return sum(min(part, 4 - part) for part in step)
-
-
-flat_steps = sorted(
-    [(dy, dx) for dy in range(4) for dx in range(4) if (dy, dx) != (0, 0)], key=hops, reverse=True
-)
+flat_steps = [(dy, dx) for dy in (2, 1, 3, 0) for dx in (2, 1, 3, 0) if (dy, dx) != (0, 0)]
 deep_steps = (2, 1, 3)
 
 
@@ -69,7 +63,7 @@
     out, refs = refs[0], refs[1:]
     held, refs = refs[:24], refs[24:]
     (
-        tok_s, seg_s, loaded,
+        tok_s, seg_s, loaded, ready,
         state, tstage, stage, taken, ea, targets_in, source, gathered,
         weights, gram, tg, u, z, xhat, rstd, zn, sb, pb, tb,
         hist, many, wa, xi, ri, zr, sr, pr, x, dx, dz1, gr, gb,
@@ -92,7 +86,9 @@
     flat_from = [at_step(4 - dy, 4 - dx) for dy, dx in flat_steps]
 
     barrier = pltpu.get_barrier_semaphore()
-    for peer in flat + deep + [partner]:
+    line_x = [(at_step(0, d), narrow) for d in deep_steps]
+    line_y = [(at_step(d, 0), narrow) for d in deep_steps]
+    for peer in line_y + line_x + deep + [partner]:
         pl.semaphore_signal(barrier, inc=1, device_id=peer, device_id_type=MESH)
 
     loads = [pltpu.make_async_copy(a, b, loaded.at[k]) for k, (a, b) in enumerate(zip(inputs, held))]
@@ -123,7 +119,7 @@
     for load in loads:
         load.wait()
     tok_v, seg_v, tgt = held[0:3]
-    for kind in range(3):
+    def keep(kind):
         emb, ab, outer, tri, mix, dist, gain = held[3 + 7 * kind : 10 + 7 * kind]
         state[kind, 0:8, :] = outer[...]
         for m in range(5):
@@ -133,6 +129,8 @@
         state[kind, 14:15, 64:66] = gain[...]
         state[kind, 16:24, 0:vocab] = emb[...]
         state[kind, 24:32, 0:64] = ab[...]
+
+    keep(0)
     ea[0:8, 0:vocab] = rounded(held[3][...])
     ea[0:8, 64:128] = rounded(held[4][...])
     low = state[0, 0:16, :].astype(bf16)
@@ -143,7 +141,9 @@
         stage[m, 0:16, :] = low
         stage[m, 16:32, :] = tstage[m].astype(bf16)
         stage[m, 32:48, :] = low_ea
-    pl.semaphore_wait(barrier, 1 + len(deep) + len(flat))
+    pl.semaphore_wait(barrier, 1 + len(deep) + len(line_x) + len(line_y))
+    for peer in line_x:
+        pl.semaphore_signal(ready, inc=1, device_id=peer, device_id_type=MESH)
 
     copies = start(
         [
@@ -152,6 +152,8 @@
         ]
     )
     taken[depth] = stage[depth]
+    keep(1)
+    keep(2)
     wait(copies)
     for m in range(depth_size):
         source[16 * m : 16 * m + 16, :] = taken[m, 0:16, :]
@@ -159,6 +161,7 @@
     source[64:96, :] = jnp.concatenate(
         [taken[m, 32:48, :].astype(f32)[0:8] for m in range(depth_size)], axis=0
     ).astype(bf16)
+    pl.semaphore_wait(ready, len(line_x))
     wide_copies = start(
         [
             remote(source, gathered.at[core, wide], sg.at[k], rg.at[k], peer)
@@ -379,17 +382,17 @@
 
     blocks = [dzt[kinds * t : kinds * t + kinds, :] for t in range(groups)]
     blocks += [dzr[kinds * i : kinds * i + kinds, :] for i in range(own_rows)]
-    dz_high, dz_low = halves(jnp.concatenate(blocks, axis=1))
-    grad_u = dot(b, dz_high, 0, 0) + dot(b, dz_low, 0, 0)
+    dz_all = jnp.concatenate(blocks, axis=1).astype(bf16)
+    grad_u = dot(b, dz_all, 0, 0)
     for t in range(parts_all):
         du[32 * t : 32 * t + 32, :] = grad_u[:, 128 * t : 128 * t + 128]
     du[32 * parts_all :, :] = jnp.zeros((32 * (48 - parts_all), 128), f32)
-    grad_b = dot(dz_high, u_all, 1, 1) + dot(dz_low, u_all, 1, 1)
-    du_high, du_low = halves(
-        jnp.concatenate([du[pl.ds(q, 48, stride=32), :] for q in range(32)], axis=1)
-    )
-    grad_outer = dot(a, du_high, 0, 0) + dot(a, du_low, 0, 0)
-    grad_a_high, grad_a_low = halves(dot(du_high, w_outer, 1, 1) + dot(du_low, w_outer, 1, 1))
+    grad_b = dot(dz_all, u_all, 1, 1)
+    du_all = jnp.concatenate(
+        [du[pl.ds(q, 48, stride=32), :] for q in range(32)], axis=1
+    ).astype(bf16)
+    grad_outer = dot(a, du_all, 0, 0)
+    grad_a_high, grad_a_low = halves(dot(du_all, w_outer, 1, 1))
     grad_a = dot(pick, grad_a_high, 0, 0) + dot(pick, grad_a_low, 0, 0)
 
     grads[...] = jnp.zeros_like(grads)
@@ -415,14 +418,14 @@
         d_block[side, 0:8, 64:96] = values[32:40]
     d_block[0, 0:1, 96:97] = loss
 
-    wait(
-        start(
-            [
-                remote(packed.at[1 - core], other, s1, r1, partner),
-                remote(d_block.at[1 - core], d_other, s2, r2, partner),
-            ]
+    d_copies = start([remote(d_block.at[1 - core], d_other, s2, r2, partner)])
+    core_copies = []
+    for k, dy in enumerate((2, 1, 3, 0)):
+        at = pl.ds(lax.rem(row + dy, 4) * 4, 4)
+        core_copies += start(
+            [remote(packed.at[1 - core, at], other.at[at], s1.at[k], r1.at[k], partner)]
         )
-    )
+    wait(d_copies)
     lane = lax.broadcasted_iota(jnp.int32, (16, 128), 1)
 
     def split_loss(block):
@@ -436,6 +439,8 @@
     small = split_loss(d_block[core] + d_other[...])
     copies = []
     for k, peer in enumerate(flat):
+        if k in (0, 4, 8, 12):
+            core_copies[k // 4].wait()
         sent[peer[0], 0:64, :] = (
             packed[core, peer[0]].astype(f32) + other[peer[0]].astype(f32)
         ).astype(bf16)
@@ -559,6 +564,7 @@
             *[VMEM(arg.shape, arg.dtype) for arg in args],
             pltpu.SMEM(args[0].shape, jnp.int32), pltpu.SMEM(args[1].shape, jnp.int32),
             pltpu.SemaphoreType.DMA((26,)),
+            pltpu.SemaphoreType.REGULAR,
             VMEM((3, 32, 128), f32),
             VMEM((depth_size, 16, 128), f32),
             VMEM((depth_size, 48, 128), bf16),
@@ -600,7 +606,7 @@
             VMEM((wide_size, 8, 128), f32),
             VMEM((8, 128), f32), VMEM((8, 128), f32),
             *sems(depth_size), *sems(wide_size), *one(), *sems(wide_size),
-            *one(), *one(), *sems(wide_size), *sems(depth_size), *one(), *sems(wide_size), *one(),
+            *sems(4), *one(), *sems(wide_size), *sems(depth_size), *one(), *sems(wide_size), *one(),
         ],
         compiler_params=pltpu.CompilerParams(
             collective_id=0, has_side_effects=True, vmem_limit_bytes=LIMIT

time: 50.3 us -> 48 us (0.954)
  Pallas kernels: 49.4 us -> 47.1 us
    pallas_call x1, Pallas kernels: 47.9 us -> 45.5 us  [step_call(): pl.pallas_call(step_kernel, out_shape=shape(104, 128), in_specs=[pl.Block...]
where the time goes in v4:
time: 48 us; the launch traced here: 47.7 us
  Pallas kernels  47.1 us (98%)
  between operations  0.68 us (1%)
    pallas_call x1, Pallas kernels, step_call(): pl.pallas_call(step_kernel, out_shape=shape(104, 128), in_specs=[pl.Block...  45.5 us
    pallas_call x1, Pallas kernels, local(): pl.pallas_call(place_kernel, out_shape=[shape(1, 1)] * 3 + shapes * 3, in...  1.52 us

profile of v4, /device:TPU:1, one launch (start us, length us, event | category | flops | bytes accessed | tf_op | source)
XLA Modules:
  0.0 47.7 jit_solution(14693968676627004118)
XLA Ops:
  0.7 45.5 %pair_step.1.stepped = f32[104,128]{1,0:T(8,128)} custom-call(s32[4,384]{1,0:T(4,128)} %refs_0_.1, s32[4,384]{1,0:T(4,128)} %refs_1_.1, s32[4,24,48]{2,1,0:T(8,128)} %refs_2_.1, f32[8,33]{1,0:T(8,128)} %bitcast.15, f32[8,64]{1,0:T(8,128)} %refs_4_.1, f32[8,128]{1,0:T(8,128)} %refs_5_.1, f32[1,640]{1,0:T(1,128)} %refs_6_.1, f32[1,128]{1,0:T(1,128)} %refs_7_.1, ...), custom_call_target="tpu_custom_call" | custom-call | tf_op jit(solution)/shard_map/pair_step/pallas_call | solution.py:558
  46.2 1.5 %place_outputs.1 = (f32[1,1]{1,0:T(1,128)}, f32[1,1]{1,0:T(1,128)}, f32[1,1]{1,0:T(1,128)}, f32[8,33]{1,0:T(8,128)}, f32[8,64]{1,0:T(8,128)}, /*index=5*/f32[8,1...) custom-call(f32[104,128]{1,0:T(8,128)} %pair_step.1.stepped), custom_call_target="tpu_custom_call" | custom-call | tf_op jit(solution)/shard_map/place_outputs/pallas_call | solution.py:624

commit v5 on v4

--- a/solution.py
+++ b/solution.py
@@ -26,6 +26,8 @@
 kinds = 40
 groups = 34
 table = groups * kinds
+side_by_side = 4
+columns_by = 4
 own_rows = 12
 own = own_rows * kinds
 parts_all = groups + own_rows
@@ -67,9 +69,9 @@
         state, tstage, stage, taken, ea, targets_in, source, gathered,
         weights, gram, tg, u, z, xhat, rstd, zn, sb, pb, tb,
         hist, many, wa, xi, ri, zr, sr, pr, x, dx, dz1, gr, gb,
-        dpt, dpr, dzt, dzr, du, grads, packed, other, sent, taken_w, sum_z, taken_z,
-        d_block, d_other, d_final, d_partner, d_all, square, squares, square_c, square_p,
-        sz, rz, sg, rg, st, rt, sc, rc, s1, r1, s2, r2, s3, r3, s5, r5, s7, r7, s8, r8, s9, r9,
+        dpt, dpr, du, grads, packed, other, sent, taken_w, sum_z, taken_z,
+        d_block, d_other, d_final, d_partner, d_all, square, squares,
+        sz, rz, sg, rg, st, rt, sc, rc, s1, r1, s2, r2, s3, r3, s5, r5, s7, r7, s8, r8,
     ) = refs
     wide = lax.axis_index("wide")
     narrow = lax.axis_index("narrow")
@@ -80,7 +82,8 @@
     def at_step(dy, dx):
         return lax.rem(row + dy, 4) * 4 + lax.rem(column + dx, 4)
 
-    partner = (wide, depth * 2 + 1 - core)
+    across = depth * 2 + 1 - core
+    partner = (wide, across)
     deep = [(wide, lax.rem(depth + k, depth_size) * 2 + core) for k in deep_steps]
     flat = [(at_step(dy, dx), narrow) for dy, dx in flat_steps]
     flat_from = [at_step(4 - dy, 4 - dx) for dy, dx in flat_steps]
@@ -174,6 +177,10 @@
         [remote(source, gathered.at[core, wide], sc.at[0], rc.at[0], partner)]
     )
 
+    tb[table:, :] = jnp.zeros((kinds * kinds - table, 128), f32)
+    gb[vocab * kinds :, :] = jnp.zeros((table - vocab * kinds, 128), f32)
+    du[32 * parts_all :, :] = jnp.zeros((32 * (48 - parts_all), 128), f32)
+    grads[pl.ds(15, 128, stride=16), :] = jnp.zeros((128, 128), f32)
     wait(moved)
     for m in range(depth_size):
         for side in range(2):
@@ -203,19 +210,22 @@
         count = count + members * members
     count = jnp.sum(count, axis=0, keepdims=True)
 
+    def unpack(side, m):
+        for deep_at in range(depth_size):
+            at = pl.ds(pl.multiple_of(16 * (8 * m + 2 * deep_at + side), 16), 16)
+            weights[at, :] = gathered[side, m, 16 * deep_at : 16 * deep_at + 16, :].astype(f32)
+
+    unpack(core, wide)
     for k in reversed(range(wide_size - 1)):
         wide_copies[k].wait_recv()
         slot = gathered.at[core, flat_from[k]]
         core_copies += start([remote(slot, slot, sc.at[k + 1], rc.at[k + 1], partner)])
-    for copy in wide_copies:
+        unpack(core, flat_from[k])
+    for copy, m in zip(core_copies, [wide] + flat_from[::-1]):
+        copy.wait_recv()
+        unpack(1 - core, m)
+    for copy in wide_copies + core_copies:
         copy.wait_send()
-    wait(core_copies)
-
-    for side in range(2):
-        for m in range(wide_size):
-            for deep_at in range(depth_size):
-                at = 16 * (8 * m + 2 * deep_at + side)
-                weights[at : at + 16, :] = gathered[side, m, 16 * deep_at : 16 * deep_at + 16, :].astype(f32)
     shards = gathered[:, :, 64:96, :].reshape(2 * wide_size * 32, 128)
     gram[...] = dot(shards, shards, 0, 0)
     a = dot(pick, gram[0:kinds, 64:96].astype(bf16), 1, 0).astype(bf16)
@@ -240,34 +250,27 @@
         u[pl.ds(q, 48, stride=32), :] = u_q[:, 128 * q : 128 * q + 128]
     u_all = jnp.concatenate([u[32 * t : 32 * t + 32, :] for t in range(parts_all)], axis=1).astype(bf16)
     z_cat = dot(b, u_all, 1, 0)
-    for t in range(parts_all):
-        z[kinds * t : kinds * t + kinds, :] = z_cat[:, 128 * t : 128 * t + 128]
-
-    chunk = 272
-    tb[table:, :] = jnp.zeros((kinds * kinds - table, 128), f32)
-
-    def forward(step, carry):
-        at = pl.ds(pl.multiple_of(step * chunk, 16), chunk)
-        values = z[at, :]
-        center = values - jnp.mean(values, -1, keepdims=True)
-        inverse = lax.rsqrt(jnp.mean(center * center, -1, keepdims=True) + norm_eps)
-        scaled = center * inverse
-        normed = (scaled * gain_in).astype(bf16)
-        xhat[at, :] = scaled
-        rstd[at, :] = jnp.broadcast_to(inverse, scaled.shape)
-        zn[at, :] = normed
-        projected = dot(normed, w_other, 1, 0)
-        gate = jax.nn.sigmoid(projected[:, 0:128])
-        value = projected[:, 128:256]
-        sb[at, :] = gate
-        pb[at, :] = value
-        tb[at, :] = rounded(gate * value)
-        return carry
-
-    lax.fori_loop(0, table // chunk, forward, 0, unroll=True)
-
-    values = z[table:, :]
-    center = values - jnp.mean(values, -1, keepdims=True)
+    pairs = jnp.concatenate([z_cat[:, 128 * t : 128 * t + 128] for t in range(groups)], axis=0)
+    own_pairs = jnp.concatenate(
+        [z_cat[:, 128 * t : 128 * t + 128] for t in range(groups, parts_all)], axis=0
+    )
+    z[...] = own_pairs
+
+    center = pairs - jnp.mean(pairs, -1, keepdims=True)
+    inverse = lax.rsqrt(jnp.mean(center * center, -1, keepdims=True) + norm_eps)
+    scaled = center * inverse
+    normed = (scaled * gain_in).astype(bf16)
+    xhat[...] = scaled
+    rstd[...] = jnp.broadcast_to(inverse, scaled.shape)
+    zn[...] = normed
+    projected = dot(normed, w_other, 1, 0)
+    gate = jax.nn.sigmoid(projected[:, 0:128])
+    value = projected[:, 128:256]
+    sb[...] = gate
+    pb[...] = value
+    tb[0:table, :] = rounded(gate * value)
+
+    center = own_pairs - jnp.mean(own_pairs, -1, keepdims=True)
     inverse = lax.rsqrt(jnp.mean(center * center, -1, keepdims=True) + norm_eps)
     scaled = center * inverse
     xi[...] = scaled
@@ -282,8 +285,8 @@
     wa[...] = many[...] * rounded(gate * value)
     gate_out = jax.nn.sigmoid(projected[:, 256:384])
 
-    for group in range(own_rows // 4):
-        mine = range(4 * group, 4 * group + 4)
+    for group in range(own_rows // columns_by):
+        mine = range(columns_by * group, columns_by * group + columns_by)
 
         def product(v, sums, mine=mine):
             edge = tb[pl.ds(v, kinds, stride=kinds), :]
@@ -291,7 +294,9 @@
                 total + wa[pl.ds(kinds * i + v, 1), :] * edge for total, i in zip(sums, mine)
             )
 
-        sums = lax.fori_loop(0, vocab, product, (jnp.zeros((kinds, 128), f32),) * 4, unroll=11)
+        sums = lax.fori_loop(
+            0, vocab, product, (jnp.zeros((kinds, 128), f32),) * columns_by, unroll=33
+        )
         for total, i in zip(sums, mine):
             x[kinds * i : kinds * i + kinds, :] = total
 
@@ -301,7 +306,7 @@
     scaled = center * inverse
     mixed = (scaled * gain_mid).astype(bf16)
     branch = dot(mixed, w_mix, 1, 0)
-    update = (z[table:, :] + gate_out * branch).astype(bf16)
+    update = (z[...] + gate_out * branch).astype(bf16)
     logits = dot(update, dist_t, 1, 1)
     top = jnp.max(logits, -1, keepdims=True)
     powers = jnp.exp(logits - top)
@@ -326,24 +331,24 @@
         - scaled * jnp.mean(grad_hat * scaled, -1, keepdims=True)
     )
 
-    gb[...] = jnp.zeros_like(gb)
-    for group in range(own_rows // 4):
-        mine = range(4 * group, 4 * group + 4)
-        weighted = [wa[kinds * i : kinds * i + kinds, :] for i in mine]
-
-        def edges(t, sums, mine=mine, weighted=weighted):
+    for group in range(own_rows // side_by_side):
+        mine = range(side_by_side * group, side_by_side * group + side_by_side)
+
+        def edges(t, sums, mine=mine, group=group):
             at = pl.ds(pl.multiple_of(t * kinds, 8), kinds)
             edge = tb[at, :]
-            right = gb[at, :]
+            right = gb[at, :] if group else jnp.zeros((kinds, 128), f32)
             news = []
-            for total, i, left in zip(sums, mine, weighted):
+            for total, i in zip(sums, mine):
                 grad = dx[pl.ds(kinds * i + t, 1), :]
                 news.append(total + grad * edge)
-                right = right + grad * left
+                right = right + grad * wa[kinds * i : kinds * i + kinds, :]
             gb[at, :] = right
             return tuple(news)
 
-        sums = lax.fori_loop(0, vocab, edges, (jnp.zeros((kinds, 128), f32),) * 4, unroll=11)
+        sums = lax.fori_loop(
+            0, vocab, edges, (jnp.zeros((kinds, 128), f32),) * side_by_side, unroll=33
+        )
         for total, i in zip(sums, mine):
             here = slice(kinds * i, kinds * i + kinds)
             gr[here, :] = total * many[here, :]
@@ -363,30 +368,25 @@
     grad_normed = dot(dpr[...], w_own, 1, 1)
     scaled = xi[...]
     grad_gain_in = jnp.sum(grad_normed * scaled, axis=0, keepdims=True)
-    dzr[...] = dz1[...] + norm_back(grad_normed, scaled, ri[...])
+    grad_own = dz1[...] + norm_back(grad_normed, scaled, ri[...])
     grad_tri_own = dot(zr[...], dpr[...], 0, 0)
 
-    def backward(step, grad_gain):
-        at = pl.ds(pl.multiple_of(step * chunk, 16), chunk)
-        gate = sb[at, :]
-        grad = gb[at, :] * gate
-        dpt[at, 0:128] = (grad * pb[at, :] * (1.0 - gate)).astype(bf16)
-        dpt[at, 128:256] = grad.astype(bf16)
-        grad_normed = dot(dpt[at, :], w_other, 1, 1)
-        scaled = xhat[at, :]
-        dzt[at, :] = norm_back(grad_normed, scaled, rstd[at, :])
-        return grad_gain + jnp.sum(grad_normed * scaled, axis=0, keepdims=True)
-
-    grad_gain_in = lax.fori_loop(0, table // chunk, backward, grad_gain_in, unroll=True)
+    gate = sb[...]
+    grad = gb[...] * gate
+    dpt[:, 0:128] = (grad * pb[...] * (1.0 - gate)).astype(bf16)
+    dpt[:, 128:256] = grad.astype(bf16)
+    grad_normed = dot(dpt[...], w_other, 1, 1)
+    scaled = xhat[...]
+    grad_table = norm_back(grad_normed, scaled, rstd[...])
+    grad_gain_in = grad_gain_in + jnp.sum(grad_normed * scaled, axis=0, keepdims=True)
     grad_tri_other = dot(zn[...], dpt[...], 0, 0)
 
-    blocks = [dzt[kinds * t : kinds * t + kinds, :] for t in range(groups)]
-    blocks += [dzr[kinds * i : kinds * i + kinds, :] for i in range(own_rows)]
+    blocks = [grad_table[kinds * t : kinds * t + kinds, :] for t in range(groups)]
+    blocks += [grad_own[kinds * i : kinds * i + kinds, :] for i in range(own_rows)]
     dz_all = jnp.concatenate(blocks, axis=1).astype(bf16)
     grad_u = dot(b, dz_all, 0, 0)
     for t in range(parts_all):
         du[32 * t : 32 * t + 32, :] = grad_u[:, 128 * t : 128 * t + 128]
-    du[32 * parts_all :, :] = jnp.zeros((32 * (48 - parts_all), 128), f32)
     grad_b = dot(dz_all, u_all, 1, 1)
     du_all = jnp.concatenate(
         [du[pl.ds(q, 48, stride=32), :] for q in range(32)], axis=1
@@ -395,7 +395,6 @@
     grad_a_high, grad_a_low = halves(dot(du_all, w_outer, 1, 1))
     grad_a = dot(pick, grad_a_high, 0, 0) + dot(pick, grad_a_low, 0, 0)
 
-    grads[...] = jnp.zeros_like(grads)
     for q in range(32):
         grads[pl.ds(16 * (q // 8) + q % 8, 32, stride=64), :] = grad_outer[:, 128 * q : 128 * q + 128]
     for at, m in enumerate((0, 1, 4)):
@@ -466,12 +465,17 @@
     for m in range(1, depth_size):
         total = total + taken_z[m].astype(f32)
     square[...] = jnp.broadcast_to(whole_sum(total[0:64] * total[0:64]), square.shape)
-    copies = start(
-        [remote(square, squares.at[wide], s8.at[k], r8.at[k], peer) for k, peer in enumerate(flat)]
-    )
+    copies = []
+    for k, peer in enumerate(flat + [(wide, narrow)]):
+        for other_core, device in enumerate((narrow, across)):
+            if k < wide_size - 1 or other_core:
+                at = 2 * k + other_core
+                copies += start(
+                    [remote(square, squares.at[core, wide], s8.at[at], r8.at[at], (peer[0], device))]
+                )
     d_final[...] = total[64:80]
     d_copies = start([remote(d_final, d_partner, s7, r7, partner)])
-    squares[wide] = square[...]
+    squares[core, wide] = square[...]
     grads[0:64, :] = total[0:64]
 
     wait(d_copies)
@@ -501,12 +505,10 @@
     first_part = beta_one * state[1]
     second_part = beta_two * state[2]
     wait(copies)
-    total = squares[0]
+    total = squares[0, 0] + squares[1, 0]
     for m in range(1, wide_size):
-        total = total + squares[m]
-    square_c[...] = total
-    wait(start([remote(square_c, square_p, s9, r9, partner)]))
-    norm = jnp.sqrt(square_c[0:1, 0:1] + square_p[0:1, 0:1] + extra)
+        total = total + (squares[0, m] + squares[1, m])
+    norm = jnp.sqrt(total[0:1, 0:1] + extra)
     clipped = grad[0:32, :] * jnp.minimum(1.0, clip_level / norm)
     moment = first_part + (1.0 - beta_one) * clipped
     speed = second_part + (1.0 - beta_two) * clipped * clipped
@@ -577,7 +579,7 @@
             VMEM((128, 128), f32),
             VMEM((16, length), f32),
             VMEM((32 * 48, 128), f32),
-            VMEM((kinds * parts_all, 128), f32),
+            VMEM((own, 128), f32),
             full, full,
             VMEM((table, 128), bf16),
             full, full,
@@ -589,8 +591,6 @@
             full,
             VMEM((table, 256), bf16),
             VMEM((own, 384), bf16),
-            full,
-            mine,
             VMEM((32 * 48, 128), f32),
             VMEM((2048, 128), f32),
             VMEM((2, wide_size, 64, 128), bf16),
@@ -603,10 +603,9 @@
             block, block, block,
             VMEM((kinds, 64), f32),
             VMEM((8, 128), f32),
-            VMEM((wide_size, 8, 128), f32),
-            VMEM((8, 128), f32), VMEM((8, 128), f32),
+            VMEM((2, wide_size, 8, 128), f32),
             *sems(depth_size), *sems(wide_size), *one(), *sems(wide_size),
-            *sems(4), *one(), *sems(wide_size), *sems(depth_size), *one(), *sems(wide_size), *one(),
+            *sems(4), *one(), *sems(wide_size), *sems(depth_size), *one(), *sems(2 * wide_size),
         ],
         compiler_params=pltpu.CompilerParams(
             collective_id=0, has_side_effects=True, vmem_limit_bytes=LIMIT

time: 48 us -> 46.7 us (0.973)
  Pallas kernels: 47.1 us -> 45.8 us
    pallas_call x1, Pallas kernels: 45.5 us -> 44.3 us  [step_call(): pl.pallas_call(step_kernel, out_shape=shape(104, 128), in_specs=[pl.Block...]
where the time goes in v5:
time: 46.7 us; the launch traced here: 46.5 us
  Pallas kernels  45.8 us (98%)
  between operations  0.68 us (1%)
    pallas_call x1, Pallas kernels, step_call(): pl.pallas_call(step_kernel, out_shape=shape(104, 128), in_specs=[pl.Block...  44.3 us
    pallas_call x1, Pallas kernels, local(): pl.pallas_call(place_kernel, out_shape=[shape(1, 1)] * 3 + shapes * 3, in...  1.52 us

profile of v5, /device:TPU:1, one launch (start us, length us, event | category | flops | bytes accessed | tf_op | source)
XLA Modules:
  0.0 46.5 jit_solution(14545540604740985520)
XLA Ops:
  0.7 44.3 %pair_step.1.stepped = f32[104,128]{1,0:T(8,128)} custom-call(s32[4,384]{1,0:T(4,128)} %refs_0_.1, s32[4,384]{1,0:T(4,128)} %refs_1_.1, s32[4,24,48]{2,1,0:T(8,128)} %refs_2_.1, f32[8,33]{1,0:T(8,128)} %bitcast.15, f32[8,64]{1,0:T(8,128)} %refs_4_.1, f32[8,128]{1,0:T(8,128)} %refs_5_.1, f32[1,640]{1,0:T(1,128)} %refs_6_.1, f32[1,128]{1,0:T(1,128)} %refs_7_.1, ...), custom_call_target="tpu_custom_call" | custom-call | tf_op jit(solution)/shard_map/pair_step/pallas_call | solution.py:560
  45.0 1.5 %place_outputs.1 = (f32[1,1]{1,0:T(1,128)}, f32[1,1]{1,0:T(1,128)}, f32[1,1]{1,0:T(1,128)}, f32[8,33]{1,0:T(8,128)}, f32[8,64]{1,0:T(8,128)}, /*index=5*/f32[8,1...) custom-call(f32[104,128]{1,0:T(8,128)} %pair_step.1.stepped), custom_call_target="tpu_custom_call" | custom-call | tf_op jit(solution)/shard_map/place_outputs/pallas_call | solution.py:623

commit v6 on v5

--- a/solution.py
+++ b/solution.py
@@ -26,6 +26,7 @@
 kinds = 40
 groups = 34
 table = groups * kinds
+pitch = 40
 side_by_side = 4
 columns_by = 4
 own_rows = 12
@@ -67,9 +68,9 @@
     (
         tok_s, seg_s, loaded, ready,
         state, tstage, stage, taken, ea, targets_in, source, gathered,
-        weights, gram, tg, u, z, xhat, rstd, zn, sb, pb, tb,
+        outer_rows, other_rows, gram, tg, u, z, xhat, rstd, zn, sb, pb, tb,
         hist, many, wa, xi, ri, zr, sr, pr, x, dx, dz1, gr, gb,
-        dpt, dpr, du, grads, packed, other, sent, taken_w, sum_z, taken_z,
+        dpt, dpr, du, outer_grads, other_grads, packed, other, sent, taken_w, sum_z, taken_z,
         d_block, d_other, d_final, d_partner, d_all, square, squares,
         sz, rz, sg, rg, st, rt, sc, rc, s1, r1, s2, r2, s3, r3, s5, r5, s7, r7, s8, r8,
     ) = refs
@@ -179,8 +180,8 @@
 
     tb[table:, :] = jnp.zeros((kinds * kinds - table, 128), f32)
     gb[vocab * kinds :, :] = jnp.zeros((table - vocab * kinds, 128), f32)
-    du[32 * parts_all :, :] = jnp.zeros((32 * (48 - parts_all), 128), f32)
-    grads[pl.ds(15, 128, stride=16), :] = jnp.zeros((128, 128), f32)
+    du[pitch * parts_all :, :] = jnp.zeros((pitch * (48 - parts_all), 128), f32)
+    other_grads[pl.ds(7, 128, stride=8), :] = jnp.zeros((128, 128), f32)
     wait(moved)
     for m in range(depth_size):
         for side in range(2):
@@ -212,8 +213,11 @@
 
     def unpack(side, m):
         for deep_at in range(depth_size):
-            at = pl.ds(pl.multiple_of(16 * (8 * m + 2 * deep_at + side), 16), 16)
-            weights[at, :] = gathered[side, m, 16 * deep_at : 16 * deep_at + 16, :].astype(f32)
+            values = gathered[side, m, 16 * deep_at : 16 * deep_at + 16, :].astype(f32)
+            at = pitch * (2 * m + deep_at // 2) + 8 * (2 * (deep_at % 2) + side)
+            outer_rows[pl.ds(pl.multiple_of(at, 8), 8), :] = values[0:8]
+            at = 8 * (8 * m + 2 * deep_at + side)
+            other_rows[pl.ds(pl.multiple_of(at, 8), 8), :] = values[8:16]
 
     unpack(core, wide)
     for k in reversed(range(wide_size - 1)):
@@ -221,34 +225,39 @@
         slot = gathered.at[core, flat_from[k]]
         core_copies += start([remote(slot, slot, sc.at[k + 1], rc.at[k + 1], partner)])
         unpack(core, flat_from[k])
-    for copy, m in zip(core_copies, [wide] + flat_from[::-1]):
-        copy.wait_recv()
-        unpack(1 - core, m)
+    shards = gathered[core, :, 64:96, :].reshape(wide_size * 32, 128)
+    products = dot(shards, shards, 0, 0)
+    order = [wide] + flat_from[::-1]
+    for first, last in ((0, 12), (12, 16)):
+        for copy, m in zip(core_copies[first:last], order[first:last]):
+            copy.wait_recv()
+            unpack(1 - core, m)
+        shards = jnp.concatenate([gathered[1 - core, m, 64:96, :] for m in order[first:last]], axis=0)
+        products = products + dot(shards, shards, 0, 0)
+    gram[...] = products
     for copy in wide_copies + core_copies:
         copy.wait_send()
-    shards = gathered[:, :, 64:96, :].reshape(2 * wide_size * 32, 128)
-    gram[...] = dot(shards, shards, 0, 0)
     a = dot(pick, gram[0:kinds, 64:96].astype(bf16), 1, 0).astype(bf16)
     b = gram[0:kinds, 96:128].astype(bf16)
     w_outer = jnp.concatenate(
-        [weights[pl.ds(16 * (q // 8) + q % 8, 32, stride=64), :] for q in range(32)], axis=1
+        [outer_rows[pl.ds(q, 32, stride=pitch), :] for q in range(32)], axis=1
     ).astype(bf16)
     w_own = jnp.concatenate(
-        [weights[pl.ds(8 + m, 128, stride=16), :] for m in (0, 1, 4)], axis=1
+        [other_rows[pl.ds(m, 128, stride=8), :] for m in (0, 1, 4)], axis=1
     ).astype(bf16)
     w_other = jnp.concatenate(
-        [weights[pl.ds(8 + m, 128, stride=16), :] for m in (2, 3)], axis=1
+        [other_rows[pl.ds(m, 128, stride=8), :] for m in (2, 3)], axis=1
     ).astype(bf16)
-    w_mix = weights[pl.ds(13, 128, stride=16), :].astype(bf16)
-    tail_t = weights[pl.ds(14, 128, stride=16), :].T
+    w_mix = other_rows[pl.ds(5, 128, stride=8), :].astype(bf16)
+    tail_t = other_rows[pl.ds(6, 128, stride=8), :].T
     dist_t = tail_t[0:bins, :].astype(bf16)
     gain_in = tail_t[64:65, :]
     gain_mid = tail_t[65:66, :]
 
     u_q = rounded(dot(a, w_outer, 1, 0))
     for q in range(32):
-        u[pl.ds(q, 48, stride=32), :] = u_q[:, 128 * q : 128 * q + 128]
-    u_all = jnp.concatenate([u[32 * t : 32 * t + 32, :] for t in range(parts_all)], axis=1).astype(bf16)
+        u[pl.ds(q, 48, stride=pitch), :] = u_q[:, 128 * q : 128 * q + 128]
+    u_all = jnp.concatenate([u[pitch * t : pitch * t + 32, :] for t in range(parts_all)], axis=1).astype(bf16)
     z_cat = dot(b, u_all, 1, 0)
     pairs = jnp.concatenate([z_cat[:, 128 * t : 128 * t + 128] for t in range(groups)], axis=0)
     own_pairs = jnp.concatenate(
@@ -386,30 +395,33 @@
     dz_all = jnp.concatenate(blocks, axis=1).astype(bf16)
     grad_u = dot(b, dz_all, 0, 0)
     for t in range(parts_all):
-        du[32 * t : 32 * t + 32, :] = grad_u[:, 128 * t : 128 * t + 128]
+        du[pitch * t : pitch * t + 32, :] = grad_u[:, 128 * t : 128 * t + 128]
     grad_b = dot(dz_all, u_all, 1, 1)
     du_all = jnp.concatenate(
-        [du[pl.ds(q, 48, stride=32), :] for q in range(32)], axis=1
+        [du[pl.ds(q, 48, stride=pitch), :] for q in range(32)], axis=1
     ).astype(bf16)
     grad_outer = dot(a, du_all, 0, 0)
     grad_a_high, grad_a_low = halves(dot(du_all, w_outer, 1, 1))
     grad_a = dot(pick, grad_a_high, 0, 0) + dot(pick, grad_a_low, 0, 0)
 
     for q in range(32):
-        grads[pl.ds(16 * (q // 8) + q % 8, 32, stride=64), :] = grad_outer[:, 128 * q : 128 * q + 128]
+        outer_grads[pl.ds(q, 32, stride=pitch), :] = grad_outer[:, 128 * q : 128 * q + 128]
     for at, m in enumerate((0, 1, 4)):
-        grads[pl.ds(8 + m, 128, stride=16), :] = grad_tri_own[:, 128 * at : 128 * at + 128]
+        other_grads[pl.ds(m, 128, stride=8), :] = grad_tri_own[:, 128 * at : 128 * at + 128]
     for at, m in enumerate((2, 3)):
-        grads[pl.ds(8 + m, 128, stride=16), :] = grad_tri_other[:, 128 * at : 128 * at + 128]
-    grads[pl.ds(13, 128, stride=16), :] = grad_mix
-    grads[pl.ds(14, 128, stride=16), :] = jnp.concatenate(
+        other_grads[pl.ds(m, 128, stride=8), :] = grad_tri_other[:, 128 * at : 128 * at + 128]
+    other_grads[pl.ds(5, 128, stride=8), :] = grad_mix
+    other_grads[pl.ds(6, 128, stride=8), :] = jnp.concatenate(
         [grad_dist_t, grad_gain_in, grad_gain_mid, jnp.zeros((62, 128), f32)], axis=0
     ).T
     for side in range(2):
         for m in range(wide_size):
             for deep_at in range(depth_size):
-                at = 16 * (8 * m + 2 * deep_at + side)
-                packed[side, m, 16 * deep_at : 16 * deep_at + 16, :] = grads[at : at + 16, :].astype(bf16)
+                at = pitch * (2 * m + deep_at // 2) + 8 * (2 * (deep_at % 2) + side)
+                values = [outer_grads[at : at + 8, :]]
+                at = 8 * (8 * m + 2 * deep_at + side)
+                values.append(other_grads[at : at + 8, :])
+                packed[side, m, 16 * deep_at : 16 * deep_at + 16, :] = jnp.concatenate(values, axis=0).astype(bf16)
     d_block[...] = jnp.zeros_like(d_block)
     for side, values in ((0, grad_a), (1, grad_b)):
         d_block[side, :, 0:32] = values[0:16]
@@ -476,7 +488,7 @@
     d_final[...] = total[64:80]
     d_copies = start([remote(d_final, d_partner, s7, r7, partner)])
     squares[core, wide] = square[...]
-    grads[0:64, :] = total[0:64]
+    other_grads[0:64, :] = total[0:64]
 
     wait(d_copies)
     highest = lax.Precision.HIGHEST
@@ -489,7 +501,7 @@
         d_all[32:40, at] = values[0:8, 64:96]
     d_total = d_all[...]
     grad = x
-    grad[0:16, :] = grads[pl.ds(pl.multiple_of(depth * 16, 16), 16), :]
+    grad[0:16, :] = other_grads[pl.ds(pl.multiple_of(depth * 16, 16), 16), :]
     grad[16:32, :] = jnp.zeros((16, 128), f32)
     grad[16:24, 0:kinds] = dot(ea[0:8, 64:128], d_total, 1, 1, highest)
     grad[24:32, 0:64] = dot(ea[0:8, 0:kinds], d_total, 1, 0, highest)
@@ -575,10 +587,10 @@
             VMEM((2, depth_size, 16, 128), bf16),
             VMEM((96, 128), bf16),
             VMEM((2, wide_size, 96, 128), bf16),
-            VMEM((2048, 128), f32),
+            VMEM((32 * pitch, 128), f32), VMEM((1024, 128), f32),
             VMEM((128, 128), f32),
             VMEM((16, length), f32),
-            VMEM((32 * 48, 128), f32),
+            VMEM((pitch * 48, 128), f32),
             VMEM((own, 128), f32),
             full, full,
             VMEM((table, 128), bf16),
@@ -591,8 +603,8 @@
             full,
             VMEM((table, 256), bf16),
             VMEM((own, 384), bf16),
-            VMEM((32 * 48, 128), f32),
-            VMEM((2048, 128), f32),
+            VMEM((pitch * 48, 128), f32),
+            VMEM((32 * pitch, 128), f32), VMEM((1024, 128), f32),
             VMEM((2, wide_size, 64, 128), bf16),
             VMEM((wide_size, 64, 128), bf16),
             VMEM((wide_size, 80, 128), bf16),

time: 46.7 us -> 45.6 us (0.976)
  Pallas kernels: 45.8 us -> 44.7 us
    pallas_call x1, Pallas kernels: 44.3 us -> 43.1 us  [step_call(): pl.pallas_call(step_kernel, out_shape=shape(104, 128), in_specs=[pl.Block...]
where the time goes in v6:
time: 45.6 us; the launch traced here: 45.3 us
  Pallas kernels  44.7 us (98%)
  between operations  0.68 us (1%)
    pallas_call x1, Pallas kernels, step_call(): pl.pallas_call(step_kernel, out_shape=shape(104, 128), in_specs=[pl.Block...  43.1 us
    pallas_call x1, Pallas kernels, local(): pl.pallas_call(place_kernel, out_shape=[shape(1, 1)] * 3 + shapes * 3, in...  1.52 us

profile of v6, /device:TPU:1, one launch (start us, length us, event | category | flops | bytes accessed | tf_op | source)
XLA Modules:
  0.0 45.3 jit_solution(2629037776186464257)
XLA Ops:
  0.7 43.1 %pair_step.1.stepped = f32[104,128]{1,0:T(8,128)} custom-call(s32[4,384]{1,0:T(4,128)} %refs_0_.1, s32[4,384]{1,0:T(4,128)} %refs_1_.1, s32[4,24,48]{2,1,0:T(8,128)} %refs_2_.1, f32[8,33]{1,0:T(8,128)} %bitcast.15, f32[8,64]{1,0:T(8,128)} %refs_4_.1, f32[8,128]{1,0:T(8,128)} %refs_5_.1, f32[1,640]{1,0:T(1,128)} %refs_6_.1, f32[1,128]{1,0:T(1,128)} %refs_7_.1, ...), custom_call_target="tpu_custom_call" | custom-call | tf_op jit(solution)/shard_map/pair_step/pallas_call | solution.py:572
  43.8 1.5 %place_outputs.1 = (f32[1,1]{1,0:T(1,128)}, f32[1,1]{1,0:T(1,128)}, f32[1,1]{1,0:T(1,128)}, f32[8,33]{1,0:T(8,128)}, f32[8,64]{1,0:T(8,128)}, /*index=5*/f32[8,1...) custom-call(f32[104,128]{1,0:T(8,128)} %pair_step.1.stepped), custom_call_target="tpu_custom_call" | custom-call | tf_op jit(solution)/shard_map/place_outputs/pallas_call | solution.py:635

commit v7 on v6

--- a/solution.py
+++ b/solution.py
@@ -54,7 +54,7 @@
 
 
 def whole_sum(values):
-    return jnp.sum(jnp.sum(values, axis=1, keepdims=True), axis=0, keepdims=True)
+    return jnp.sum(jnp.sum(values, axis=0, keepdims=True), axis=1, keepdims=True)
 
 
 flat_steps = [(dy, dx) for dy in (2, 1, 3, 0) for dx in (2, 1, 3, 0) if (dy, dx) != (0, 0)]
@@ -225,18 +225,13 @@
         slot = gathered.at[core, flat_from[k]]
         core_copies += start([remote(slot, slot, sc.at[k + 1], rc.at[k + 1], partner)])
         unpack(core, flat_from[k])
-    shards = gathered[core, :, 64:96, :].reshape(wide_size * 32, 128)
-    products = dot(shards, shards, 0, 0)
-    order = [wide] + flat_from[::-1]
-    for first, last in ((0, 12), (12, 16)):
-        for copy, m in zip(core_copies[first:last], order[first:last]):
-            copy.wait_recv()
-            unpack(1 - core, m)
-        shards = jnp.concatenate([gathered[1 - core, m, 64:96, :] for m in order[first:last]], axis=0)
-        products = products + dot(shards, shards, 0, 0)
-    gram[...] = products
+    for copy, m in zip(core_copies, [wide] + flat_from[::-1]):
+        copy.wait_recv()
+        unpack(1 - core, m)
     for copy in wide_copies + core_copies:
         copy.wait_send()
+    shards = gathered[:, :, 64:96, :].reshape(2 * wide_size * 32, 128)
+    gram[...] = dot(shards, shards, 0, 0)
     a = dot(pick, gram[0:kinds, 64:96].astype(bf16), 1, 0).astype(bf16)
     b = gram[0:kinds, 96:128].astype(bf16)
     w_outer = jnp.concatenate(
@@ -614,8 +609,8 @@
             VMEM((2, 16, 128), f32),
             block, block, block,
             VMEM((kinds, 64), f32),
-            VMEM((8, 128), f32),
-            VMEM((2, wide_size, 8, 128), f32),
+            VMEM((1, 128), f32),
+            VMEM((2, wide_size, 1, 128), f32),
             *sems(depth_size), *sems(wide_size), *one(), *sems(wide_size),
             *sems(4), *one(), *sems(wide_size), *sems(depth_size), *one(), *sems(2 * wide_size),
         ],

time: 45.6 us -> 45.2 us (level)
  no operation moved by 1% of the time
where the time goes in v7:
time: 45.2 us; the launch traced here: 45 us
  Pallas kernels  44.3 us (98%)
  between operations  0.68 us (2%)
    pallas_call x1, Pallas kernels, step_call(): pl.pallas_call(step_kernel, out_shape=shape(104, 128), in_specs=[pl.Block...  42.8 us
    pallas_call x1, Pallas kernels, local(): pl.pallas_call(place_kernel, out_shape=[shape(1, 1)] * 3 + shapes * 3, in...  1.52 us

profile of v7, /device:TPU:1, one launch (start us, length us, event | category | flops | bytes accessed | tf_op | source)
XLA Modules:
  0.0 45.0 jit_solution(15455583580399281321)
XLA Ops:
  0.7 42.8 %pair_step.1.stepped = f32[104,128]{1,0:T(8,128)} custom-call(s32[4,384]{1,0:T(4,128)} %refs_0_.1, s32[4,384]{1,0:T(4,128)} %refs_1_.1, s32[4,24,48]{2,1,0:T(8,128)} %refs_2_.1, f32[8,33]{1,0:T(8,128)} %bitcast.15, f32[8,64]{1,0:T(8,128)} %refs_4_.1, f32[8,128]{1,0:T(8,128)} %refs_5_.1, f32[1,640]{1,0:T(1,128)} %refs_6_.1, f32[1,128]{1,0:T(1,128)} %refs_7_.1, ...), custom_call_target="tpu_custom_call" | custom-call | tf_op jit(solution)/shard_map/pair_step/pallas_call | solution.py:567
  43.4 1.5 %place_outputs.1 = (f32[1,1]{1,0:T(1,128)}, f32[1,1]{1,0:T(1,128)}, f32[1,1]{1,0:T(1,128)}, f32[8,33]{1,0:T(8,128)}, f32[8,64]{1,0:T(8,128)}, /*index=5*/f32[8,1...) custom-call(f32[104,128]{1,0:T(8,128)} %pair_step.1.stepped), custom_call_target="tpu_custom_call" | custom-call | tf_op jit(solution)/shard_map/place_outputs/pallas_call | solution.py:630

commit v8 on v7

--- a/solution.py
+++ b/solution.py
@@ -98,7 +98,8 @@
     loads = [pltpu.make_async_copy(a, b, loaded.at[k]) for k, (a, b) in enumerate(zip(inputs, held))]
     loads.append(pltpu.make_async_copy(inputs[0], tok_s, loaded.at[24]))
     loads.append(pltpu.make_async_copy(inputs[1], seg_s, loaded.at[25]))
-    for load in loads:
+    urgent, later = loads[2:10], loads[0:2] + loads[10:]
+    for load in urgent + later:
         load.start()
 
     def remote(source_ref, target_ref, send, receive, peer):
@@ -120,7 +121,7 @@
     tstage[...] = jnp.zeros_like(tstage)
     stage[...] = jnp.zeros_like(stage)
     ea[...] = jnp.zeros_like(ea)
-    for load in loads:
+    for load in urgent:
         load.wait()
     tok_v, seg_v, tgt = held[0:3]
     def keep(kind):
@@ -156,6 +157,8 @@
         ]
     )
     taken[depth] = stage[depth]
+    for load in later:
+        load.wait()
     keep(1)
     keep(2)
     wait(copies)
@@ -385,6 +388,15 @@
     grad_gain_in = grad_gain_in + jnp.sum(grad_normed * scaled, axis=0, keepdims=True)
     grad_tri_other = dot(zn[...], dpt[...], 0, 0)
 
+    for at, m in enumerate((0, 1, 4)):
+        other_grads[pl.ds(m, 128, stride=8), :] = grad_tri_own[:, 128 * at : 128 * at + 128]
+    for at, m in enumerate((2, 3)):
+        other_grads[pl.ds(m, 128, stride=8), :] = grad_tri_other[:, 128 * at : 128 * at + 128]
+    other_grads[pl.ds(5, 128, stride=8), :] = grad_mix
+    other_grads[pl.ds(6, 128, stride=8), :] = jnp.concatenate(
+        [grad_dist_t, grad_gain_in, grad_gain_mid, jnp.zeros((62, 128), f32)], axis=0
+    ).T
+
     blocks = [grad_table[kinds * t : kinds * t + kinds, :] for t in range(groups)]
     blocks += [grad_own[kinds * i : kinds * i + kinds, :] for i in range(own_rows)]
     dz_all = jnp.concatenate(blocks, axis=1).astype(bf16)
@@ -401,14 +413,6 @@
 
     for q in range(32):
         outer_grads[pl.ds(q, 32, stride=pitch), :] = grad_outer[:, 128 * q : 128 * q + 128]
-    for at, m in enumerate((0, 1, 4)):
-        other_grads[pl.ds(m, 128, stride=8), :] = grad_tri_own[:, 128 * at : 128 * at + 128]
-    for at, m in enumerate((2, 3)):
-        other_grads[pl.ds(m, 128, stride=8), :] = grad_tri_other[:, 128 * at : 128 * at + 128]
-    other_grads[pl.ds(5, 128, stride=8), :] = grad_mix
-    other_grads[pl.ds(6, 128, stride=8), :] = jnp.concatenate(
-        [grad_dist_t, grad_gain_in, grad_gain_mid, jnp.zeros((62, 128), f32)], axis=0
-    ).T
     for side in range(2):
         for m in range(wide_size):
             for deep_at in range(depth_size):

time: 45.2 us -> 45.2 us (level)
  no operation moved by 1% of the time
where the time goes in v8:
time: 45.2 us; the launch traced here: 45 us
  Pallas kernels  44.3 us (98%)
  between operations  0.68 us (2%)
    pallas_call x1, Pallas kernels, step_call(): pl.pallas_call(step_kernel, out_shape=shape(104, 128), in_specs=[pl.Block...  42.8 us
    pallas_call x1, Pallas kernels, local(): pl.pallas_call(place_kernel, out_shape=[shape(1, 1)] * 3 + shapes * 3, in...  1.52 us

profile of v8, /device:TPU:1, one launch (start us, length us, event | category | flops | bytes accessed | tf_op | source)
XLA Modules:
  0.0 45.0 jit_solution(12533945334413878378)
XLA Ops:
  0.7 42.8 %pair_step.1.stepped = f32[104,128]{1,0:T(8,128)} custom-call(s32[4,384]{1,0:T(4,128)} %refs_0_.1, s32[4,384]{1,0:T(4,128)} %refs_1_.1, s32[4,24,48]{2,1,0:T(8,128)} %refs_2_.1, f32[8,33]{1,0:T(8,128)} %bitcast.15, f32[8,64]{1,0:T(8,128)} %refs_4_.1, f32[8,128]{1,0:T(8,128)} %refs_5_.1, f32[1,640]{1,0:T(1,128)} %refs_6_.1, f32[1,128]{1,0:T(1,128)} %refs_7_.1, ...), custom_call_target="tpu_custom_call" | custom-call | tf_op jit(solution)/shard_map/pair_step/pallas_call | solution.py:571
  43.4 1.5 %place_outputs.1 = (f32[1,1]{1,0:T(1,128)}, f32[1,1]{1,0:T(1,128)}, f32[1,1]{1,0:T(1,128)}, f32[8,33]{1,0:T(8,128)}, f32[8,64]{1,0:T(8,128)}, /*index=5*/f32[8,1...) custom-call(f32[104,128]{1,0:T(8,128)} %pair_step.1.stepped), custom_call_target="tpu_custom_call" | custom-call | tf_op jit(solution)/shard_map/place_outputs/pallas_call | solution.py:634
